TPU v7x, 32 devices: a whole 2x2x4 slice. The times are simulated.
32 devices in a mesh: seq: 8 (over z, x), fsdp: 4 (over y, core).
Axes of the slice: x: 2, y: 2, z: 4, core: 2. Of those that a mesh axis runs over, the one named last changes fastest.
Arguments:
- hidden_in: bfloat16 [4, 2048, 1024], P('fsdp', 'seq'), may hold values from -24 to 24
- cotangent: float32 [4, 2048, 1024], P('fsdp', 'seq'), may hold values from -6 to 6
- gains: float32 [2, 3072], P(None, 'fsdp'), may hold values from 0.5 to 1.5
- gains_first: float32 [2, 3072], P(None, 'fsdp'), may hold values from -64 to 64
- gains_second: float32 [2, 3072], P(None, 'fsdp'), may hold values from 245.76 to 2457.6
- in_proj: float32 [2, 1024, 4384], P(None, 'fsdp'), may hold values from -0.1875 to 0.1875
- in_proj_first: float32 [2, 1024, 4384], P(None, 'fsdp'), may hold values from -32 to 32
- in_proj_second: float32 [2, 1024, 4384], P(None, 'fsdp'), may hold values from 61.44 to 614.4
- conv_taps: float32 [2, 5, 2304], P(None, None, 'fsdp'), may hold values from -3 to 3
- conv_taps_first: float32 [2, 5, 2304], P(None, None, 'fsdp'), may hold values from -32 to 32
- conv_taps_second: float32 [2, 5, 2304], P(None, None, 'fsdp'), may hold values from 61.44 to 614.4
- head_params: float32 [2, 3, 32], P(None, None, 'fsdp'), may hold values from -9 to 1.5
- head_params_first: float32 [2, 3, 32], P(None, None, 'fsdp'), may hold values from -192 to 192
- head_params_second: float32 [2, 3, 32], P(None, None, 'fsdp'), may hold values from 2211.84 to 22118.4
- out_proj: float32 [2, 2048, 1024], P(None, 'fsdp'), may hold values from -0.125 to 0.125
- out_proj_first: float32 [2, 2048, 1024], P(None, 'fsdp'), may hold values from -64 to 64
- out_proj_second: float32 [2, 2048, 1024], P(None, 'fsdp'), may hold values from 245.76 to 2457.6
Outputs:
- hidden_out: float32 [4, 2048, 1024], P('fsdp', 'seq')
- hidden_grad: float32 [4, 2048, 1024], P('fsdp', 'seq')
- gains_first_new: float32 [2, 3072], P(None, 'fsdp')
- gains_second_new: float32 [2, 3072], P(None, 'fsdp')
- gains_new: float32 [2, 3072], P(None, 'fsdp')
- in_proj_first_new: float32 [2, 1024, 4384], P(None, 'fsdp')
- in_proj_second_new: float32 [2, 1024, 4384], P(None, 'fsdp')
- in_proj_new: float32 [2, 1024, 4384], P(None, 'fsdp')
- conv_taps_first_new: float32 [2, 5, 2304], P(None, None, 'fsdp')
- conv_taps_second_new: float32 [2, 5, 2304], P(None, None, 'fsdp')
- conv_taps_new: float32 [2, 5, 2304], P(None, None, 'fsdp')
- head_params_first_new: float32 [2, 3, 32], P(None, None, 'fsdp')
- head_params_second_new: float32 [2, 3, 32], P(None, None, 'fsdp')
- head_params_new: float32 [2, 3, 32], P(None, None, 'fsdp')
- out_proj_first_new: float32 [2, 2048, 1024], P(None, 'fsdp')
- out_proj_second_new: float32 [2, 2048, 1024], P(None, 'fsdp')
- out_proj_new: float32 [2, 2048, 1024], P(None, 'fsdp')
All inputs are finite; a program needn't handle non-finite values.
Results may differ from a plain program's by a relative error of at most 0.025.
The roundings to bfloat16 on the way count: a program that leaves them out, or rounds other values in their place, can miss the bound.
Values may be sent and summed in bfloat16 or wider, within the bound.
A program may use at most 320 MiB of HBM per device.

v0:
```python
import jax
import jax.numpy as jnp
from jax import lax
from jax.sharding import PartitionSpec as P

D = 1024
H = 32
TAPS = 4
SPAN = 256
LAYERS = 2
STEP = 10
DI = 2048
CH = 2304


highest = lax.Precision.HIGHEST
norm_eps = 1e-05
beta_one = 0.9
beta_two = 0.95
adam_eps = 1e-08
learn_rates = (0.4, 0.06, 0.5, 3.0, 0.05)
weight_decays = (0.0, 0.1, 0.0, 0.0, 0.1)


def rounded(values):
    return lax.optimization_barrier(values.astype(jnp.bfloat16)).astype(jnp.float32)


def rms_norm(values, gain_vec):
    mean_sq = jnp.mean(values * values, axis=-1, keepdims=True)
    return values * lax.rsqrt(mean_sq + norm_eps) * gain_vec


def gate_piece(mixed_out, gate_cols, gain_vec):
    return rms_norm(mixed_out * jax.nn.silu(gate_cols), gain_vec)


def causal_conv(signal, taps_bias, rim_vals):
    padded = jnp.concatenate([rim_vals, signal], axis=1)
    tap_count = taps_bias.shape[0] - 1
    tok_count = signal.shape[1]
    summed = jnp.zeros_like(signal) + taps_bias[tap_count]
    for tap_idx in range(tap_count):
        summed = summed + padded[:, tap_idx : tap_idx + tok_count, :] * taps_bias[tap_idx]
    return jax.nn.silu(summed)


def ssd_blocks(x_heads, step_size, log_decay, b_state, c_state):
    tok_count, head_count, head_width = x_heads.shape
    states = b_state.shape[1]
    groups = tok_count // SPAN
    positions = jnp.arange(SPAN)
    causal = (positions[:, None] >= positions[None, :]).astype(jnp.float32)

    def one_block(state_carry, block_items):
        x_blk, step_blk, decay_blk, b_blk, c_blk = block_items
        cumulative = jnp.cumsum(decay_blk, axis=0)
        log_gaps = cumulative[:, None, :] - cumulative[None, :, :]
        kernel = jnp.exp(log_gaps * causal[:, :, None]) * causal[:, :, None]
        inner_prod = jnp.dot(c_blk, b_blk.T, precision=highest)
        mixing = kernel * inner_prod[:, :, None] * step_blk[None, :, :]
        within = jnp.einsum("tsh,shp->thp", mixing, x_blk, precision=highest)
        from_carry = jnp.exp(cumulative)[:, :, None] * jnp.einsum(
            "tn,hpn->thp", c_blk, state_carry, precision=highest
        )
        tail_weight = jnp.exp(cumulative[-1][None, :] - cumulative) * step_blk
        carry_next = jnp.exp(cumulative[-1])[:, None, None] * state_carry + jnp.einsum(
            "shp,sn->hpn", x_blk * tail_weight[:, :, None], b_blk, precision=highest
        )
        return (carry_next, within + from_carry)

    block_items = (
        x_heads.reshape(groups, SPAN, head_count, head_width),
        step_size.reshape(groups, SPAN, head_count),
        log_decay.reshape(groups, SPAN, head_count),
        b_state.reshape(groups, SPAN, states),
        c_state.reshape(groups, SPAN, states),
    )
    state_start = jnp.zeros((head_count, head_width, states), jnp.float32)
    final_state, outputs = lax.scan(jax.checkpoint(one_block), state_start, block_items)
    return (
        outputs.reshape(tok_count, head_count, head_width),
        final_state,
        jnp.sum(log_decay, axis=0),
    )


def mixer_piece(x_act, step_raw, bc_act, head_vals):
    batch_seqs, tok_count, chan_count = x_act.shape
    head_count = step_raw.shape[2]
    states = bc_act.shape[2] // 2
    x_heads = x_act.reshape(batch_seqs, tok_count, head_count, chan_count // head_count)
    step_size = jax.nn.softplus(step_raw + head_vals[0])
    log_decay = -jnp.exp(head_vals[1]) * step_size
    outputs, finals, totals = jax.vmap(ssd_blocks)(
        x_heads, step_size, log_decay, bc_act[:, :, :states], bc_act[:, :, states:]
    )
    outputs = outputs + head_vals[2][:, None] * x_heads
    return (outputs.reshape(batch_seqs, tok_count, chan_count), finals, totals)


def adam_step(weight, first_old, second_old, grad_vals, learn_rate, decay_rate):
    first_new = beta_one * first_old + (1.0 - beta_one) * grad_vals
    second_new = beta_two * second_old + (1.0 - beta_two) * grad_vals * grad_vals
    first_hat = first_new / (1.0 - beta_one**STEP)
    second_hat = second_new / (1.0 - beta_two**STEP)
    weight_new = weight - learn_rate * (
        first_hat / (jnp.sqrt(second_hat) + adam_eps) + decay_rate * weight
    )
    return (first_new, second_new, weight_new)


def local(
    hidden_in,
    cotangent,
    gains,
    gains_first,
    gains_second,
    in_proj,
    in_proj_first,
    in_proj_second,
    conv_taps,
    conv_taps_first,
    conv_taps_second,
    head_params,
    head_params_first,
    head_params_second,
    out_proj,
    out_proj_first,
    out_proj_second,
):
    masters = (gains, in_proj, conv_taps, head_params, out_proj)
    firsts = (gains_first, in_proj_first, conv_taps_first, head_params_first, out_proj_first)
    seconds = (gains_second, in_proj_second, conv_taps_second, head_params_second, out_proj_second)
    seq_index = lax.axis_index("seq")
    batch_seqs, tok_count, feature_dim = hidden_in.shape
    rim_len = TAPS - 1
    hidden = hidden_in.astype(jnp.float32)
    saved_layers = []
    for layer_idx in range(LAYERS):
        fetched = (
            lax.all_gather(gains[layer_idx].astype(jnp.bfloat16), "fsdp", axis=0, tiled=True),
            lax.all_gather(in_proj[layer_idx].astype(jnp.bfloat16), "fsdp", axis=0, tiled=True),
            lax.all_gather(conv_taps[layer_idx].astype(jnp.bfloat16), "fsdp", axis=1, tiled=True),
            lax.all_gather(head_params[layer_idx].astype(jnp.bfloat16), "fsdp", axis=1, tiled=True),
            lax.all_gather(out_proj[layer_idx].astype(jnp.bfloat16), "fsdp", axis=0, tiled=True),
        )
        gain_vals = fetched[0].astype(jnp.float32)
        conv_vals = fetched[2].astype(jnp.float32)
        head_vals = fetched[3].astype(jnp.float32)
        normed, pull_norm = jax.vjp(rms_norm, hidden, gain_vals[:D])
        normed_b = normed.astype(jnp.bfloat16)
        projected = jnp.einsum(
            "std,de->ste", normed_b, fetched[1], preferred_element_type=jnp.float32
        ).astype(jnp.bfloat16)
        gate_cols = projected[:, :, :DI]
        conv_in = projected[:, :, DI : DI + CH]
        step_pre = projected[:, :, DI + CH :]
        x_part, step_part = (
            lax.all_to_all(conv_in[:, :, :DI], "seq", split_axis=2, concat_axis=1, tiled=True),
            lax.all_to_all(step_pre, "seq", split_axis=2, concat_axis=1, tiled=True),
        )
        bc_part = lax.all_gather(conv_in[:, :, DI:], "seq", axis=1, tiled=True)
        own_chans = x_part.shape[2]
        own_heads = step_part.shape[2]
        conv_own = jnp.concatenate(
            [
                lax.dynamic_slice_in_dim(conv_vals, seq_index * own_chans, own_chans, 1),
                conv_vals[:, DI:],
            ],
            axis=1,
        )
        head_own = lax.dynamic_slice_in_dim(head_vals, seq_index * own_heads, own_heads, 1)
        signal = jnp.concatenate([x_part, bc_part], axis=2).astype(jnp.float32)
        rim_zero = jnp.zeros((batch_seqs, rim_len, signal.shape[2]), jnp.float32)
        conv_out, pull_conv = jax.vjp(causal_conv, signal, conv_own, rim_zero)
        x_act = rounded(conv_out[:, :, :own_chans])
        bc_act = rounded(conv_out[:, :, own_chans:])
        mixer_outs, pull_mixer = jax.vjp(
            mixer_piece, x_act, step_part.astype(jnp.float32), bc_act, head_own
        )
        mixed_tok = lax.all_to_all(
            mixer_outs[0].astype(jnp.bfloat16), "seq", split_axis=1, concat_axis=2, tiled=True
        )
        mixer_state = (pull_conv, pull_mixer, own_chans, own_heads, mixer_outs[1], mixer_outs[2])
        normed_gate, pull_gate = jax.vjp(
            gate_piece, mixed_tok.astype(jnp.float32), gate_cols.astype(jnp.float32), gain_vals[D:]
        )
        normed_gate_b = normed_gate.astype(jnp.bfloat16)
        branch = jnp.einsum(
            "ste,ed->std", normed_gate_b, fetched[4], preferred_element_type=jnp.float32
        )
        saved_layers.append((fetched, pull_norm, normed_b, pull_gate, normed_gate_b, mixer_state))
        hidden = hidden + branch
    grad_stream = cotangent
    layer_grads = []
    for layer_idx in reversed(range(LAYERS)):
        fetched_fwd, pull_norm, normed_b, pull_gate, normed_gate_b, mixer_state = saved_layers[
            layer_idx
        ]
        fetched = (
            lax.all_gather(gains[layer_idx].astype(jnp.bfloat16), "fsdp", axis=0, tiled=True),
            lax.all_gather(in_proj[layer_idx].astype(jnp.bfloat16), "fsdp", axis=0, tiled=True),
            lax.all_gather(conv_taps[layer_idx].astype(jnp.bfloat16), "fsdp", axis=1, tiled=True),
            lax.all_gather(head_params[layer_idx].astype(jnp.bfloat16), "fsdp", axis=1, tiled=True),
            lax.all_gather(out_proj[layer_idx].astype(jnp.bfloat16), "fsdp", axis=0, tiled=True),
        )
        grad_branch = grad_stream.astype(jnp.bfloat16)
        grad_out_mat = jnp.einsum(
            "ste,std->ed", normed_gate_b, grad_branch, preferred_element_type=jnp.float32
        )
        grad_normed_gate = jnp.einsum(
            "std,ed->ste", grad_branch, fetched[4], preferred_element_type=jnp.float32
        )
        grad_mixed, grad_gate, grad_gain_two = pull_gate(grad_normed_gate)
        grad_mixed_b = grad_mixed.astype(jnp.bfloat16)
        pull_conv, pull_mixer, own_chans, own_heads, finals, totals = mixer_state
        grad_heads = lax.all_to_all(grad_mixed_b, "seq", split_axis=2, concat_axis=1, tiled=True)
        grad_x_act, grad_step, grad_bc_act, grad_head_own = pull_mixer(
            (grad_heads.astype(jnp.float32), jnp.zeros_like(finals), jnp.zeros_like(totals))
        )
        grad_signal, grad_conv_own, grad_rim = pull_conv(
            jnp.concatenate([grad_x_act, grad_bc_act], axis=2)
        )
        grad_x_tok, grad_step_tok = (
            lax.all_to_all(
                grad_signal[:, :, :own_chans].astype(jnp.bfloat16),
                "seq",
                split_axis=1,
                concat_axis=2,
                tiled=True,
            ),
            lax.all_to_all(
                grad_step.astype(jnp.bfloat16), "seq", split_axis=1, concat_axis=2, tiled=True
            ),
        )
        grad_bc_tok = lax.psum_scatter(
            grad_signal[:, :, own_chans:].astype(jnp.bfloat16),
            "seq",
            scatter_dimension=1,
            tiled=True,
        )
        grad_proj = jnp.concatenate(
            [grad_gate.astype(jnp.bfloat16), grad_x_tok, grad_bc_tok, grad_step_tok], axis=2
        )
        grad_conv_x = lax.dynamic_update_slice_in_dim(
            jnp.zeros((TAPS + 1, DI), jnp.float32),
            grad_conv_own[:, :own_chans],
            seq_index * own_chans,
            1,
        )
        grad_conv = jnp.concatenate([grad_conv_x, grad_conv_own[:, own_chans:]], axis=1)
        grad_head = lax.dynamic_update_slice_in_dim(
            jnp.zeros((3, H), jnp.float32), grad_head_own, seq_index * own_heads, 1
        )
        grad_in_mat = jnp.einsum(
            "std,ste->de", normed_b, grad_proj, preferred_element_type=jnp.float32
        )
        grad_normed = jnp.einsum(
            "ste,de->std", grad_proj, fetched[1], preferred_element_type=jnp.float32
        )
        grad_hidden, grad_gain_one = pull_norm(grad_normed)
        grad_stream = grad_stream + grad_hidden
        grad_gain_all = jnp.concatenate([grad_gain_one, grad_gain_two])
        reduced = (
            lax.psum_scatter(
                grad_gain_all.astype(jnp.bfloat16), "fsdp", scatter_dimension=0, tiled=True
            ).astype(jnp.float32),
            lax.psum_scatter(
                grad_in_mat.astype(jnp.bfloat16), "fsdp", scatter_dimension=0, tiled=True
            ).astype(jnp.float32),
            lax.psum_scatter(
                grad_conv.astype(jnp.bfloat16), "fsdp", scatter_dimension=1, tiled=True
            ).astype(jnp.float32),
            lax.psum_scatter(
                grad_head.astype(jnp.bfloat16), "fsdp", scatter_dimension=1, tiled=True
            ).astype(jnp.float32),
            lax.psum_scatter(
                grad_out_mat.astype(jnp.bfloat16), "fsdp", scatter_dimension=0, tiled=True
            ).astype(jnp.float32),
        )
        reduced = (
            lax.psum(reduced[0].astype(jnp.bfloat16), "seq").astype(jnp.float32),
            lax.psum(reduced[1].astype(jnp.bfloat16), "seq").astype(jnp.float32),
            lax.psum(reduced[2].astype(jnp.bfloat16), "seq").astype(jnp.float32),
            lax.psum(reduced[3].astype(jnp.bfloat16), "seq").astype(jnp.float32),
            lax.psum(reduced[4].astype(jnp.bfloat16), "seq").astype(jnp.float32),
        )
        layer_grads.insert(0, reduced)
    results = [hidden, grad_stream]
    for kind_idx in range(5):
        grad_stack = jnp.stack([layer_grads[layer_idx][kind_idx] for layer_idx in range(LAYERS)])
        first_new, second_new, weight_new = adam_step(
            masters[kind_idx],
            firsts[kind_idx],
            seconds[kind_idx],
            grad_stack,
            learn_rates[kind_idx],
            weight_decays[kind_idx],
        )
        results.extend([first_new, second_new, weight_new])
    return (
        results[0],
        results[1],
        results[2],
        results[3],
        results[4],
        results[5],
        results[6],
        results[7],
        results[8],
        results[9],
        results[10],
        results[11],
        results[12],
        results[13],
        results[14],
        results[15],
        results[16],
    )


def solution(mesh):
    in_specs = (
        P("fsdp", "seq", None),
        P("fsdp", "seq", None),
        P(None, "fsdp"),
        P(None, "fsdp"),
        P(None, "fsdp"),
        P(None, "fsdp", None),
        P(None, "fsdp", None),
        P(None, "fsdp", None),
        P(None, None, "fsdp"),
        P(None, None, "fsdp"),
        P(None, None, "fsdp"),
        P(None, None, "fsdp"),
        P(None, None, "fsdp"),
        P(None, None, "fsdp"),
        P(None, "fsdp", None),
        P(None, "fsdp", None),
        P(None, "fsdp", None),
    )
    out_specs = (
        P("fsdp", "seq", None),
        P("fsdp", "seq", None),
        P(None, "fsdp"),
        P(None, "fsdp"),
        P(None, "fsdp"),
        P(None, "fsdp", None),
        P(None, "fsdp", None),
        P(None, "fsdp", None),
        P(None, None, "fsdp"),
        P(None, None, "fsdp"),
        P(None, None, "fsdp"),
        P(None, None, "fsdp"),
        P(None, None, "fsdp"),
        P(None, None, "fsdp"),
        P(None, "fsdp", None),
        P(None, "fsdp", None),
        P(None, "fsdp", None),
    )
    return jax.shard_map(local, mesh=mesh, in_specs=in_specs, out_specs=out_specs, check_vma=False)
```

profile of v0, /device:TPU:0, one launch (start us, length us, event | category | flops | bytes accessed | tf_op | source)
XLA Modules:
  0.0 2308.1 jit_solution(9995981358331019105)
XLA Ops:
  21.3 58.0 %all-gather.21.cloned.1.call-done = bf16[1,1024,4384]{1,2,0:T(8,128)(2,1)} async-done(((bf16[1,256,4384]{1,2,0:T(8,128)(2,1)}), bf16[1,1024,4384]{1,2,0:T(8,128)(2,1)}) %all-gather.21.cloned.1.call-update) | async-done | bytes 8978448 | tf_op jit(solution)/shard_map/all_gather | solution.py:143
  112.1 11.7 copy.868
  141.5 17.3 all-gather.8
  194.2 138.0 %while.86 = (s32[]{:T(128)}, f32[1,4,64,128]{3,2,1,0:T(8,128)S(1)}, f32[8,1,256,4,64]{2,0,4,3,1:T(8,128)}, f32[8,1,4,64,128]{4,3,2,1,0:T(8,128)}, f32[8,1,256,4]...) while((s32[]{:T(128)}, f32[1,4,64,128]{3,2,1,0:T(8,128)S(1)}, ...), condition=%wide.region_4.6_spmd.clone.clone, body=%wide.region_1.5_spmd.clone.clone.sunk | while | flops 505252864 | bytes 4705900 | solution.py:80
  344.6 11.6 reduce.166
  368.5 21.0 all-to-all-done.2
  413.8 11.7 copy.867
  445.8 23.3 %all-to-all-done.4 = bf16[8,2,32768]{2,1,0:T(2,128)(2,1)S(1)} async-done(((bf16[8,2,32768]{2,1,0:T(2,128)(2,1)}), bf16[8,2,32768]{2,1,0:T(2,128)(2,1)S(1)}, u32[]{:S(2)}, u32[]{:S(2)}) %all-to-all-start.4) | async-done | bytes 1048608 | tf_op jit(solution)/shard_map/all_to_all | solution.py:160
  489.8 138.0 %while.87 = (s32[]{:T(128)}, f32[1,4,64,128]{3,2,1,0:T(8,128)S(1)}, f32[8,1,256,4,64]{2,0,4,3,1:T(8,128)}, f32[8,1,4,64,128]{4,3,2,1,0:T(8,128)}, f32[8,1,256,4]...) while((s32[]{:T(128)}, f32[1,4,64,128]{3,2,1,0:T(8,128)S(1)}, ...), condition=%wide.region_10.12_spmd.clone.clone, body=%wide.region_7.11_spmd.clone.clone.sunk | while | flops 505252864 | bytes 4705900 | solution.py:80
  640.1 11.6 reduce.169
  656.9 25.9 %all-to-all-done.5 = bf16[8,2,32768]{2,1,0:T(2,128)(2,1)S(1)} async-done(((bf16[8,2,32768]{2,1,0:T(2,128)(2,1)}), bf16[8,2,32768]{2,1,0:T(2,128)(2,1)S(1)}, u32[]{:S(2)}, u32[]{:S(2)}) %all-to-all-start.5) | async-done | bytes 1048608 | tf_op jit(solution)/shard_map/all_to_all | solution.py:182
  698.2 12.9 copy.866
  711.1 11.6 reduce.170
  727.9 25.5 %all-to-all-done.6 = bf16[8,2,32768]{2,1,0:T(2,128)(2,1)S(1)} async-done(((bf16[8,2,32768]{2,1,0:T(2,128)(2,1)}), bf16[8,2,32768]{2,1,0:T(2,128)(2,1)S(1)}, u32[]{:S(2)}, u32[]{:S(2)}) %all-to-all-start.6) | async-done | bytes 1048608 | tf_op jit(solution)/shard_map/all_to_all | solution.py:218
  770.4 338.0 %while.84 = (s32[]{:T(128)}, f32[1,4,64,128]{3,2,1,0:T(8,128)S(1)}, f32[8,1,256,4,64]{2,0,4,3,1:T(8,128)}, f32[8,1,256,4]{2,3,1,0:T(4,128)}, f32[8,1,256,4]{2,3,...) while((s32[]{:T(128)}, f32[1,4,64,128]{3,2,1,0:T(8,128)S(1)}, ...), condition=%wide.region_26.28_spmd.clone, body=%wide.region_13.27_spmd.clone.sunk | while | flops 1214364672 | bytes 12994391 | solution.py:80
  1143.5 13.3 reduce.171
  1166.6 11.6 reduce.172
  1190.5 24.9 %all-to-all-done.7 = bf16[8,2,32768]{2,1,0:T(2,128)(2,1)S(1)} async-done(((bf16[8,2,32768]{2,1,0:T(2,128)(2,1)}), bf16[8,2,32768]{2,1,0:T(2,128)(2,1)S(1)}, u32[]{:S(2)}, u32[]{:S(2)}) %all-to-all-start.7) | async-done | bytes 1048608 | tf_op jit(solution)/shard_map/all_to_all | solution.py:226
  1239.3 12.9 copy.865
  1268.5 25.7 %all-to-all-done.9 = bf16[8,2,32768]{2,1,0:T(2,128)(2,1)S(1)} async-done(((bf16[8,2,32768]{2,1,0:T(2,128)(2,1)}), bf16[8,2,32768]{2,1,0:T(2,128)(2,1)S(1)}, u32[]{:S(2)}, u32[]{:S(2)}) %all-to-all-start.9) | async-done | bytes 1048608 | tf_op jit(solution)/shard_map/all_to_all | solution.py:218
  1311.4 336.3 %while.85 = (s32[]{:T(128)}, f32[1,4,64,128]{3,2,1,0:T(8,128)S(1)}, f32[8,1,256,4,64]{2,0,4,3,1:T(8,128)}, f32[8,1,256,4]{2,3,1,0:T(4,128)}, f32[8,1,256,4]{2,3,...) while((s32[]{:T(128)}, f32[1,4,64,128]{3,2,1,0:T(8,128)S(1)}, ...), condition=%wide.region_43.45_spmd.clone, body=%wide.region_30.44_spmd.clone.sunk | while | flops 1214364672 | bytes 12994391 | solution.py:80
  1701.9 13.3 reduce.174
  1727.1 12.5 reduce.175
  1752.9 20.6 all-to-all-done.10
  1795.5 40.8 %reduce-scatter.23.cloned.1.call-done = bf16[512,1024]{1,0:T(8,128)(2,1)} async-done(((bf16[2048,1024]{1,0:T(8,128)(2,1)}), bf16[512,1024]{1,0:T(8,128)(2,1)}) %reduce-scatter.23.cloned.1.call-update) | async-done | bytes 1048592 | tf_op jit(solution)/shard_map/reduce_scatter | solution.py:278
  1836.2 78.7 %reduce-scatter.21.cloned.1.call-done = bf16[256,4384]{0,1:T(8,128)(2,1)} async-done(((bf16[1024,4384]{0,1:T(8,128)(2,1)}), bf16[256,4384]{0,1:T(8,128)(2,1)}) %reduce-scatter.21.cloned.1.call-update) | async-done | bytes 2244624 | tf_op jit(solution)/shard_map/reduce_scatter | solution.py:269
  1914.9 78.6 %reduce-scatter.19.cloned.1.call-done = bf16[256,4384]{0,1:T(8,128)(2,1)} async-done(((bf16[1024,4384]{0,1:T(8,128)(2,1)}), bf16[256,4384]{0,1:T(8,128)(2,1)}) %reduce-scatter.19.cloned.1.call-update) | async-done | bytes 2244624 | tf_op jit(solution)/shard_map/reduce_scatter | solution.py:269
  2001.4 17.3 reduce-scatter.29.cloned.1.call-done
  2020.1 23.6 %reduce-scatter.27.cloned.1.call-done = bf16[576,5]{1,0:T(8,128)(2,1)} async-done(((bf16[2304,5]{1,0:T(8,128)(2,1)}), bf16[576,5]{1,0:T(8,128)(2,1)}) %reduce-scatter.27.cloned.1.call-update) | async-done | bytes 5776
  2062.9 40.3 %all-reduce.38 = (bf16[1,768]{1,0:T(2,128)(2,1)S(1)}, bf16[1,768]{1,0:T(2,128)(2,1)S(1)}, bf16[1,5,576]{2,1,0:T(8,128)(2,1)S(1)}, bf16[1,5,576]{2,1,0:T(8,128)(2...) all-reduce(bf16[1,768]{1,0:T(2,128)(2,1)S(1)} %stack.71, ...), channel_id=1, replica_groups=mesh['seq'=8,'fsdp'=4] {'seq'}, use_global_device_ids=true, to_apply=%region_53.55 | all-reduce | flops 7344 | bytes 29376 | tf_op jit(solution)/shard_map/psum | solution.py:283
  2108.9 162.6 %all-reduce.43.cloned.1.call-done = (bf16[1,256,4384]{1,2,0:T(8,128)(2,1)}, bf16[1,256,4384]{1,2,0:T(8,128)(2,1)}, bf16[1,512,1024]{2,1,0:T(8,128)(2,1)}, bf16[1,512,1024]{2,1,0:T(8,128)(2,1)}) async-done(((bf16[1,256,4384]{1,2,0:T(8,128)(2,1)}, bf16[1,256,4384]{1,2,0:T(8,128)(2,1)}, bf16[1,512,1024]{2,1,0:T(8,128)(2,1)}, bf16[1,512,1024]{2,1,0:T(8,128)(2,1)}), (bf16[1,256,4384]{1,2,0:T(8,128)(2,1)}, ...) | async-done | bytes 6586384 | tf_op jit(solution)/shard_map/psum | solution.py:284
  2271.4 23.6 %multiply_subtract_fusion = (f32[2,256,4384]{1,2,0:T(8,128)}, f32[2,256,4384]{1,2,0:T(8,128)}, f32[2,256,4384]{1,2,0:T(8,128)}) fusion(f32[2,256,4384]{1,2,0:T(8,128)} %param.31, bf16[1,256,4384]{1,2,0:T(8,128)(2,1)} %get-tuple-element.1616, bf16[1,256,4384]{1,2,0:T(8,128)(2,1)} %get-tuple-element.1617, f32[2,256,4384]{1,2,0:T(8,128)} %param.33, ...), kind=kLoop, calls=%fused_computation.312 | loop fusion | flops 38158336 | bytes 58359808 | tf_op jit(solution)/shard_map/sub | solution.py:107
  (1913 shorter events, 1445.6 us)
Async XLA Ops:
  7.2 72.2 %all-gather.21.cloned.1.call-start = ((), (), s32[]{:S(2)}) async-start(), calls=%async_computation.28 | async-start | bytes 11223040 | tf_op jit(solution)/shard_map/all_gather | solution.py:143
  13.6 161.5 %all-gather.17.cloned.1.call-start = ((), (), s32[]{:S(2)}) async-start(), calls=%async_computation.20 | async-start | bytes 1179648 | tf_op jit(solution)/shard_map/all_gather | solution.py:163
  21.1 64.4 %copy-start.103 = (f32[1,1024]{1,0:T(1,128)}, f32[1,1024]{1,0:T(1,128)S(1)}, u32[]{:S(2)}) copy-start(f32[1,1024]{1,0:T(1,128)S(1)} %slice.441) | copy-start | bytes 12292
  21.3 64.2 %copy-start.111 = (f32[256]{0:T(256)}, f32[256]{0:T(256)S(1)}, u32[]{:S(2)}) copy-start(f32[256]{0:T(256)S(1)} %fusion.263) | copy-start | bytes 3076
  86.3 310.6 %all-gather.23.cloned.1.call-start = ((), (), s32[]{:S(2)}) async-start(), calls=%async_computation.29 | async-start | bytes 5242880 | tf_op jit(solution)/shard_map/all_gather | solution.py:146
  90.4 311.0 %all-gather.25.cloned.1.call-start = ((), (), s32[]{:S(2)}) async-start(), calls=%async_computation.30 | async-start | bytes 11223040 | tf_op jit(solution)/shard_map/all_gather | solution.py:143
  106.4 29.1 %all-to-all-start = ((bf16[8,2,512]{2,1,0:T(2,128)(2,1)}), bf16[8,2,512]{2,1,0:T(2,128)(2,1)S(1)}, u32[]{:S(2)}, u32[]{:S(2)}) async-start(bf16[8,2,512]{2,1,0:T(2,128)(2,1)} %reshape.2308), calls=%async_computation | async-start | bytes 32768 | tf_op jit(solution)/shard_map/all_to_all | solution.py:161
  135.5 38.1 %all-to-all-start.1 = ((bf16[8,2,32768]{2,1,0:T(2,128)(2,1)}), bf16[8,2,32768]{2,1,0:T(2,128)(2,1)S(1)}, u32[]{:S(2)}, u32[]{:S(2)}) async-start(bf16[8,2,32768]{2,1,0:T(2,128)(2,1)} %reshape.2306), calls=%async_computation.1 | async-start | bytes 2097152 | tf_op jit(solution)/shard_map/all_to_all | solution.py:160
  183.1 152.6 %copy-start.10 = (bf16[1,2048,256]{1,2,0:T(8,128)(2,1)}, bf16[1,2048,256]{1,2,0:T(8,128)(2,1)S(1)}, u32[]{:S(2)}) copy-start(bf16[1,2048,256]{1,2,0:T(8,128)(2,1)S(1)} %get-tuple-element.1716) | copy-start | bytes 3145732
  357.2 32.3 %all-to-all-start.2 = ((bf16[8,2,32768]{2,1,0:T(2,128)(2,1)}), bf16[8,2,32768]{2,1,0:T(2,128)(2,1)S(1)}, u32[]{:S(2)}, u32[]{:S(2)}) async-start(bf16[8,2,32768]{2,1,0:T(2,128)(2,1)} %reshape.2310), calls=%async_computation.2 | async-start | bytes 2097152 | tf_op jit(solution)/shard_map/all_to_all | solution.py:182
  363.3 107.6 %all-gather.19.cloned.1.call-start = ((), (), s32[]{:S(2)}) async-start(), calls=%async_computation.21 | async-start | bytes 1179648 | tf_op jit(solution)/shard_map/all_gather | solution.py:163
  410.1 27.1 %all-to-all-start.3 = ((bf16[8,2,512]{2,1,0:T(2,128)(2,1)}), bf16[8,2,512]{2,1,0:T(2,128)(2,1)S(1)}, u32[]{:S(2)}, u32[]{:S(2)}) async-start(bf16[8,2,512]{2,1,0:T(2,128)(2,1)} %reshape.2314), calls=%async_computation.3 | async-start | bytes 32768 | tf_op jit(solution)/shard_map/all_to_all | solution.py:161
  437.2 31.8 %all-to-all-start.4 = ((bf16[8,2,32768]{2,1,0:T(2,128)(2,1)}), bf16[8,2,32768]{2,1,0:T(2,128)(2,1)S(1)}, u32[]{:S(2)}, u32[]{:S(2)}) async-start(bf16[8,2,32768]{2,1,0:T(2,128)(2,1)} %reshape.2312), calls=%async_computation.4 | async-start | bytes 2097152 | tf_op jit(solution)/shard_map/all_to_all | solution.py:160
  443.2 247.0 %all-gather.27.cloned.1.call-start = ((), (), s32[]{:S(2)}) async-start(), calls=%async_computation.31 | async-start | bytes 5242880 | tf_op jit(solution)/shard_map/all_gather | solution.py:146
  444.9 186.4 %copy-start.109 = (f32[256]{0:T(256)}, f32[256]{0:T(256)S(1)}, u32[]{:S(2)}) copy-start(f32[256]{0:T(256)S(1)} %mul.1926) | copy-start | bytes 3076
  478.7 152.5 %copy-start.12 = (bf16[1,2048,256]{1,2,0:T(8,128)(2,1)}, bf16[1,2048,256]{1,2,0:T(8,128)(2,1)S(1)}, u32[]{:S(2)}) copy-start(bf16[1,2048,256]{1,2,0:T(8,128)(2,1)S(1)} %get-tuple-element.1712) | copy-start | bytes 3145732
  652.7 30.1 %all-to-all-start.5 = ((bf16[8,2,32768]{2,1,0:T(2,128)(2,1)}), bf16[8,2,32768]{2,1,0:T(2,128)(2,1)S(1)}, u32[]{:S(2)}, u32[]{:S(2)}) async-start(bf16[8,2,32768]{2,1,0:T(2,128)(2,1)} %reshape.2316), calls=%async_computation.5 | async-start | bytes 2097152 | tf_op jit(solution)/shard_map/all_to_all | solution.py:182
  723.8 29.6 %all-to-all-start.6 = ((bf16[8,2,32768]{2,1,0:T(2,128)(2,1)}), bf16[8,2,32768]{2,1,0:T(2,128)(2,1)S(1)}, u32[]{:S(2)}, u32[]{:S(2)}) async-start(bf16[8,2,32768]{2,1,0:T(2,128)(2,1)} %reshape.2318), calls=%async_computation.6 | async-start | bytes 2097152 | tf_op jit(solution)/shard_map/all_to_all | solution.py:218
  727.4 496.6 %reduce-scatter.15.cloned.1.call-start = ((), (), s32[]{:S(2)}) async-start(), calls=%async_computation.22 | async-start | bytes 1179648 | tf_op jit(solution)/shard_map/reduce_scatter | solution.py:237
  1159.2 20.1 all-to-all-start.8
  1179.3 36.2 %all-to-all-start.7 = ((bf16[8,2,32768]{2,1,0:T(2,128)(2,1)}), bf16[8,2,32768]{2,1,0:T(2,128)(2,1)S(1)}, u32[]{:S(2)}, u32[]{:S(2)}) async-start(bf16[8,2,32768]{2,1,0:T(2,128)(2,1)} %reshape.2322), calls=%async_computation.7 | async-start | bytes 2097152 | tf_op jit(solution)/shard_map/all_to_all | solution.py:226
  1264.8 29.4 %all-to-all-start.9 = ((bf16[8,2,32768]{2,1,0:T(2,128)(2,1)}), bf16[8,2,32768]{2,1,0:T(2,128)(2,1)S(1)}, u32[]{:S(2)}, u32[]{:S(2)}) async-start(bf16[8,2,32768]{2,1,0:T(2,128)(2,1)} %reshape.2324), calls=%async_computation.10 | async-start | bytes 2097152 | tf_op jit(solution)/shard_map/all_to_all | solution.py:218
  1268.4 515.9 %reduce-scatter.17.cloned.1.call-start = ((), (), s32[]{:S(2)}) async-start(), calls=%async_computation.23 | async-start | bytes 1179648 | tf_op jit(solution)/shard_map/reduce_scatter | solution.py:237
  1679.1 116.4 %reduce-scatter.25.cloned.1.call-start = ((), (), s32[]{:S(2)}) async-start(), calls=%async_computation.27 | async-start | bytes 5242880 | tf_op jit(solution)/shard_map/reduce_scatter | solution.py:278
  1682.5 153.7 %reduce-scatter.23.cloned.1.call-start = ((), (), s32[]{:S(2)}) async-start(), calls=%async_computation.26 | async-start | bytes 5242880 | tf_op jit(solution)/shard_map/reduce_scatter | solution.py:278
  1688.7 226.3 %reduce-scatter.21.cloned.1.call-start = ((), (), s32[]{:S(2)}) async-start(), calls=%async_computation.25 | async-start | bytes 11223040 | tf_op jit(solution)/shard_map/reduce_scatter | solution.py:269
  1717.6 24.2 %all-to-all-start.11 = ((bf16[8,2,512]{2,1,0:T(2,128)(2,1)}), bf16[8,2,512]{2,1,0:T(2,128)(2,1)S(1)}, u32[]{:S(2)}, u32[]{:S(2)}) async-start(bf16[8,2,512]{2,1,0:T(2,128)(2,1)} %reshape.2326), calls=%async_computation.13 | async-start | bytes 32768 | tf_op jit(solution)/shard_map/all_to_all | solution.py:233
  1741.8 31.7 %all-to-all-start.10 = ((bf16[8,2,32768]{2,1,0:T(2,128)(2,1)}), bf16[8,2,32768]{2,1,0:T(2,128)(2,1)}, u32[]{:S(2)}, u32[]{:S(2)}) async-start(bf16[8,2,32768]{2,1,0:T(2,128)(2,1)} %reshape.2328), calls=%async_computation.11 | async-start | bytes 2097152 | tf_op jit(solution)/shard_map/all_to_all | solution.py:226
  1747.8 245.7 %reduce-scatter.19.cloned.1.call-start = ((), (), s32[]{:S(2)}) async-start(), calls=%async_computation.24 | async-start | bytes 11223040 | tf_op jit(solution)/shard_map/reduce_scatter | solution.py:269
  1792.3 226.4 %reduce-scatter.29.cloned.1.call-start = ((), (), s32[]{:S(2)}) async-start(), calls=%async_computation.33 | async-start | bytes 737280
  1794.1 249.6 %reduce-scatter.27.cloned.1.call-start = ((), (), s32[]{:S(2)}) async-start(), calls=%async_computation.32 | async-start | bytes 737280
  1795.4 476.0 %all-reduce.43.cloned.1.call-start = ((), (), s32[]{:S(2)}) async-start(), calls=%async_computation.34 | async-start | bytes 13172736 | tf_op jit(solution)/shard_map/psum | solution.py:284
  (204 other events, 2068.3 us)
Sparse Core Ops, SparseCore 0:
  13.8 65.5 all-gather.20
  86.4 39.6 all-gather.16
  128.3 39.8 all-gather.22
  170.1 62.8 all-gather.24
  408.9 38.5 all-gather.18
  449.4 39.6 all-gather.26
  1140.0 64.4 reduce-scatter.14
  1679.2 62.6 reduce-scatter.16
  1745.0 43.5 reduce-scatter.24
  1791.7 44.5 reduce-scatter.22
  1839.4 75.4 reduce-scatter.20
  1918.0 75.4 reduce-scatter.18
  1996.6 22.0 reduce-scatter.28
  2021.6 22.0 reduce-scatter.26
  2048.0 223.3 all-reduce.42
where the time goes:
time: 2330 us; the launch traced here: 2310 us
  local copies, waits for them, and re-layouts  686 us (29%)
  waiting for transfers between devices  628 us (27%)
  other arithmetic  479 us (21%)
  matrix products  335 us (14%)
  blocking collectives  101 us (4%)
  starting transfers between devices  59.1 us (3%)
    dynamic_update_slice x96, local copies, waits for them, and re-layouts, ssd_blocks(): lax.scan(jax.checkpoint(one_block), state_start, block_items)  309 us
    psum x1, waiting for transfers between devices, local(): lax.psum(reduced[1].astype(jnp.bfloat16), 'seq').astype(jnp.float32)  163 us
    another operation x117, other arithmetic  161 us
    reduce_scatter x2, waiting for transfers between devices, local(): lax.psum_scatter(grad_in_mat.astype(jnp.bfloat16), 'fsdp', scatter_dimens...  157 us
    unnamed x16, other arithmetic  119 us
    dot_general x48, matrix products, one_block(): within = jnp.einsum('tsh,shp->thp', mixing, x_blk, precision=highest)  109 us
    unnamed x344, local copies, waits for them, and re-layouts  83.8 us
    squeeze x64, local copies, waits for them, and re-layouts, ssd_blocks(): lax.scan(jax.checkpoint(one_block), state_start, block_items)  58.7 us
  transfers between devices with their start and end apart: 27, of which 14 were waited for; matrix products, arithmetic and copies ran while one was open for 26% of the time, Pallas kernels for 0%

commit v1 on v0

v1 whole, which is shorter than its diff:
```python
import functools

import jax
import jax.numpy as jnp
from jax import lax
from jax.experimental import pallas as pl
from jax.experimental.pallas import tpu as pltpu
from jax.sharding import PartitionSpec as P

D = 1024
H = 32
HP = 64
STATE = 128
TAPS = 4
SPAN = 256
LAYERS = 2
STEP = 10
DI = 2048
CH = 2304
GROUP = 8
COLS = GROUP * HP

highest = lax.Precision.HIGHEST
norm_eps = 1e-05
beta_one = 0.9
beta_two = 0.95
adam_eps = 1e-08
learn_rates = (0.4, 0.06, 0.5, 3.0, 0.05)
weight_decays = (0.0, 0.1, 0.0, 0.0, 0.1)
bf16 = jnp.bfloat16
f32 = jnp.float32


def dot(a, b, ca, cb):
    return lax.dot_general(a, b, (((ca,), (cb,)), ((), ())), preferred_element_type=f32)


def head(ref, j):
    return ref[:, j * HP : (j + 1) * HP]


def state_kernel(x_ref, b_ref, w_ref, s_ref):
    w = jnp.transpose(w_ref[0])
    for j in range(GROUP):
        wx = (head(x_ref, j).astype(f32) * w[:, j : j + 1]).astype(bf16)
        s_ref[0, j * HP : (j + 1) * HP, :] = dot(wx, b_ref[...], 0, 0).astype(bf16)


def decay(cum, cum_cols, j, causal):
    gaps = cum_cols[:, j : j + 1] - cum[j : j + 1, :]
    return jnp.exp(jnp.where(causal, gaps, -1e30))


def causal_mask():
    rows = lax.broadcasted_iota(jnp.int32, (SPAN, SPAN), 0)
    cols = lax.broadcasted_iota(jnp.int32, (SPAN, SPAN), 1)
    return rows >= cols


def inner_kernel(x_ref, b_ref, c_ref, cum_ref, dt_ref, y_ref):
    causal = causal_mask()
    cb = dot(c_ref[...], b_ref[...], 1, 1)
    cum = cum_ref[0]
    dt = dt_ref[0]
    cum_cols = jnp.transpose(cum)
    for j in range(GROUP):
        mix = decay(cum, cum_cols, j, causal) * cb * dt[j : j + 1, :]
        y_ref[:, j * HP : (j + 1) * HP] = dot(mix.astype(bf16), head(x_ref, j), 1, 0)


def carry_kernel(y_ref, x_ref, c_ref, cum_ref, skip_ref, hin_ref, out_ref):
    grow = jnp.transpose(jnp.exp(cum_ref[0]))
    skip = jnp.transpose(skip_ref[0])
    for j in range(GROUP):
        rows = slice(j * HP, (j + 1) * HP)
        from_carry = dot(c_ref[...], hin_ref[0, rows, :], 1, 1) * grow[:, j : j + 1]
        skipped = head(x_ref, j).astype(f32) * skip[:, j : j + 1]
        out_ref[:, rows] = (y_ref[:, rows] + from_carry + skipped).astype(bf16)


def back_state_kernel(gy_ref, c_ref, cum_ref, g_ref):
    grow = jnp.transpose(jnp.exp(cum_ref[0]))
    for j in range(GROUP):
        egy = (head(gy_ref, j).astype(f32) * grow[:, j : j + 1]).astype(bf16)
        g_ref[0, j * HP : (j + 1) * HP, :] = dot(egy, c_ref[...], 0, 0).astype(bf16)


def back_inner_kernel(
    x_ref, gy_ref, b_ref, c_ref, cum_ref, dt_ref, skip_ref,
    gx_ref, gcb_ref, row_ref, col_ref, gskip_ref,
):
    causal = causal_mask()
    cb = dot(c_ref[...], b_ref[...], 1, 1)
    cum = cum_ref[0]
    dt = dt_ref[0]
    cum_cols = jnp.transpose(cum)
    dt_cols = jnp.transpose(dt)
    skip = jnp.transpose(skip_ref[0])

    @pl.when(pl.program_id(1) == 0)
    def _():
        gcb_ref[...] = jnp.zeros_like(gcb_ref)

    total = jnp.zeros((SPAN, SPAN), f32)
    row_list, skip_list = [], []
    for j in range(GROUP):
        e = decay(cum, cum_cols, j, causal)
        x = head(x_ref, j)
        gy = head(gy_ref, j)
        rho = dot(gy, x, 1, 1)
        e_rho = e * rho
        kept = e_rho * dt[j : j + 1, :]
        total = total + kept
        row_list.append(jnp.sum(kept * cb, axis=1, keepdims=True))
        col_ref[0, j : j + 1, :] = jnp.sum(e_rho * cb, axis=0, keepdims=True)
        gx = dot((e * cb).astype(bf16), gy, 0, 0) * dt_cols[:, j : j + 1]
        gyf = gy.astype(f32)
        gx_ref[:, j * HP : (j + 1) * HP] = gx + gyf * skip[:, j : j + 1]
        skip_list.append(jnp.sum(gyf * x.astype(f32), axis=1, keepdims=True))
    gcb_ref[0] += total
    row_ref[0] = jnp.transpose(jnp.concatenate(row_list, axis=1))
    gskip_ref[0] = jnp.transpose(jnp.concatenate(skip_list, axis=1))


def back_carry_kernel(
    gxi_ref, x_ref, gy_ref, b_ref, c_ref, cum_ref, w_ref, hin_ref, gs_ref,
    gx_ref, gb_ref, gc_ref, carry_ref, dw_ref, cross_ref,
):
    @pl.when(pl.program_id(1) == 0)
    def _():
        gb_ref[...] = jnp.zeros_like(gb_ref)
        gc_ref[...] = jnp.zeros_like(gc_ref)

    grow = jnp.transpose(jnp.exp(cum_ref[0]))
    w = jnp.transpose(w_ref[0])
    gb = jnp.zeros((SPAN, STATE), f32)
    gc = jnp.zeros((SPAN, STATE), f32)
    carry_list, dw_list = [], []
    for j in range(GROUP):
        rows = slice(j * HP, (j + 1) * HP)
        hin = hin_ref[0, rows, :]
        gs = gs_ref[0, rows, :]
        x = head(x_ref, j).astype(f32)
        egy = head(gy_ref, j).astype(f32) * grow[:, j : j + 1]
        b_gs = dot(b_ref[...], gs, 1, 1)
        c_hin = dot(c_ref[...], hin, 1, 1)
        gx_ref[:, rows] = gxi_ref[:, rows] + b_gs * w[:, j : j + 1]
        dw_list.append(jnp.sum(x * b_gs, axis=1, keepdims=True))
        carry_list.append(jnp.sum(egy * c_hin, axis=1, keepdims=True))
        gb = gb + dot((x * w[:, j : j + 1]).astype(bf16), gs, 1, 0)
        gc = gc + dot(egy.astype(bf16), hin, 1, 0)
        cross_ref[0, j : j + 1, :] = jnp.sum(hin.astype(f32) * gs.astype(f32), axis=0, keepdims=True)
    gb_ref[...] += gb
    gc_ref[...] += gc
    carry_ref[0] = jnp.transpose(jnp.concatenate(carry_list, axis=1))
    dw_ref[0] = jnp.transpose(jnp.concatenate(dw_list, axis=1))


x_spec = pl.BlockSpec((SPAN, COLS), lambda g, i: (g, i))
b_spec = pl.BlockSpec((SPAN, STATE), lambda g, i: (g, DI // STATE))
c_spec = pl.BlockSpec((SPAN, STATE), lambda g, i: (g, DI // STATE + 1))
bc_out_spec = pl.BlockSpec((SPAN, STATE), lambda g, i: (g, 0))
row_spec = pl.BlockSpec((1, GROUP, SPAN), lambda g, i: (g, i, 0))
one_spec = pl.BlockSpec((1, GROUP, 1), lambda g, i: (0, i, 0))
state_spec = pl.BlockSpec((1, COLS, STATE), lambda g, i: (g, i, 0))
gcb_spec = pl.BlockSpec((1, SPAN, SPAN), lambda g, i: (g, 0, 0))
cross_spec = pl.BlockSpec((1, GROUP, STATE), lambda g, i: (g, i, 0))


def call(kernel, name, chunks, ins, outs, flops, *args):
    shapes = [s for _, s in outs]
    moved = sum(a.size * a.dtype.itemsize for a in args)
    moved += sum(s.size * s.dtype.itemsize for s in shapes)
    return pl.pallas_call(
        kernel,
        grid=(chunks, H // GROUP),
        in_specs=ins,
        out_specs=[s for s, _ in outs],
        out_shape=shapes,
        name=name,
        compiler_params=pltpu.CompilerParams(
            dimension_semantics=("arbitrary", "arbitrary"), vmem_limit_bytes=40 * 1024 * 1024
        ),
        cost_estimate=pl.CostEstimate(
            flops=flops * chunks, bytes_accessed=moved, transcendentals=chunks * H * SPAN * SPAN
        ),
    )(*args)


def shape(dims, dtype=f32):
    return jax.ShapeDtypeStruct(dims, dtype)


small_flops = 2 * SPAN * DI * STATE
inner_flops = 20 * H * SPAN * SPAN * HP


def rms_scale(values):
    return lax.rsqrt(jnp.mean(values * values, axis=-1, keepdims=True) + norm_eps)


def silu_slope(w):
    sig = jax.nn.sigmoid(w)
    return sig * (1.0 + w * (1.0 - sig))


def adam_step(weight, first_old, second_old, grad_vals, learn_rate, decay_rate):
    first_new = beta_one * first_old + (1.0 - beta_one) * grad_vals
    second_new = beta_two * second_old + (1.0 - beta_two) * grad_vals * grad_vals
    first_hat = first_new / (1.0 - beta_one**STEP)
    second_hat = second_new / (1.0 - beta_two**STEP)
    weight_new = weight - learn_rate * (
        first_hat / (jnp.sqrt(second_hat) + adam_eps) + decay_rate * weight
    )
    return (first_new, second_new, weight_new)


def exchange(states, seqs, weights, shards, spec):
    n = states.shape[0] // seqs
    own = DI // shards
    send = states.reshape(seqs * n, shards, own, STATE)
    got = lax.all_to_all(send, "seq", split_axis=1, concat_axis=0, tiled=False)
    got = got.reshape(shards, seqs, n, own // HP, HP * STATE)
    got = got.astype(f32)
    mixed = jnp.einsum(spec, weights, got, precision=highest).astype(bf16)
    mixed = mixed.reshape(shards, seqs * n, own, STATE)
    back = lax.all_to_all(mixed, "seq", split_axis=0, concat_axis=1, tiled=False)
    return back.reshape(seqs * n, DI, STATE)


def chunk_weights(totals, seqs, shards):
    n = totals.shape[0] // seqs
    every = lax.all_gather(totals.reshape(seqs, n, H), "seq", axis=1, tiled=True)
    chunks = shards * n
    own = H // shards
    mine = lax.dynamic_slice_in_dim(every, lax.axis_index("seq") * own, own, 2)
    place = jnp.arange(chunks)
    between = (place[None, None, :] < place[:, None, None]) & (place[None, None, :] > place[None, :, None])
    logs = jnp.einsum("ijk,bkh->ijbh", between.astype(f32), mine, precision=highest)
    ahead = (place[:, None] > place[None, :])[:, :, None, None]
    weights = jnp.where(ahead, jnp.exp(jnp.where(ahead, logs, 0.0)), 0.0)
    return weights.reshape(shards, n, shards, n, seqs, own)


def local(
    hidden_in,
    cotangent,
    gains,
    gains_first,
    gains_second,
    in_proj,
    in_proj_first,
    in_proj_second,
    conv_taps,
    conv_taps_first,
    conv_taps_second,
    head_params,
    head_params_first,
    head_params_second,
    out_proj,
    out_proj_first,
    out_proj_second,
):
    masters = (gains, in_proj, conv_taps, head_params, out_proj)
    firsts = (gains_first, in_proj_first, conv_taps_first, head_params_first, out_proj_first)
    seconds = (gains_second, in_proj_second, conv_taps_second, head_params_second, out_proj_second)
    shards = lax.axis_size("seq")
    owners = lax.axis_size("fsdp")
    fsdp_index = lax.axis_index("fsdp")
    seqs, toks, _ = hidden_in.shape
    rows = seqs * toks
    n = toks // SPAN
    chunks = seqs * n
    rim = TAPS - 1
    right = [(i, i + 1) for i in range(shards - 1)]
    left = [(i + 1, i) for i in range(shards - 1)]

    smalls = jnp.concatenate(
        [gains.reshape(-1), conv_taps.reshape(-1), head_params.reshape(-1)]
    ).astype(bf16)
    smalls = lax.all_gather(smalls, "fsdp", axis=0)
    size_a = gains.size
    size_b = size_a + conv_taps.size
    gains_all = smalls[:, :size_a].reshape(owners, LAYERS, -1)
    gains_all = jnp.moveaxis(gains_all, 0, 1).reshape(LAYERS, D + DI).astype(f32)
    taps_all = smalls[:, size_a:size_b].reshape(owners, LAYERS, TAPS + 1, -1)
    taps_all = jnp.moveaxis(taps_all, 0, 2).reshape(LAYERS, TAPS + 1, CH).astype(f32)
    heads_all = smalls[:, size_b:].reshape(owners, LAYERS, 3, -1)
    heads_all = jnp.moveaxis(heads_all, 0, 2).reshape(LAYERS, 3, H).astype(f32)
    in_mats = [
        lax.all_gather(in_proj[i].astype(bf16), "fsdp", axis=0, tiled=True) for i in range(LAYERS)
    ]
    out_mats = [
        lax.all_gather(out_proj[i].astype(bf16), "fsdp", axis=0, tiled=True) for i in range(LAYERS)
    ]

    upper = (jnp.arange(SPAN)[:, None] <= jnp.arange(SPAN)[None, :]).astype(f32)

    hidden = hidden_in.astype(f32).reshape(rows, D)
    saved = []
    for i in range(LAYERS):
        g1, g2 = gains_all[i, :D], gains_all[i, D:]
        taps, heads = taps_all[i], heads_all[i]
        rs1 = rms_scale(hidden)
        u = (hidden * rs1 * g1).astype(bf16)
        proj = dot(u, in_mats[i], 1, 0).astype(bf16)
        z = proj[:, :DI]
        c = proj[:, DI : DI + CH].reshape(seqs, toks, CH)
        raw = proj[:, DI + CH :].astype(f32).reshape(chunks, SPAN, H).transpose(0, 2, 1)
        halo = lax.ppermute(c[:, toks - rim :, :], "seq", right)
        padded = jnp.concatenate([halo, c], axis=1)
        pa = taps[TAPS]
        for k in range(TAPS):
            pa = pa + padded[:, k : k + toks, :].astype(f32) * taps[k]
        pa = pa.reshape(rows, CH)
        a = (pa * jax.nn.sigmoid(pa)).astype(bf16)
        pre = raw + heads[0][:, None]
        dt = jax.nn.softplus(pre)
        rate = -jnp.exp(heads[1])
        lam = rate[:, None] * dt
        cum = jnp.einsum("ghs,st->ght", lam, upper, precision=highest)
        last = cum[:, :, SPAN - 1 :]
        tail = jnp.exp(last - cum)
        w = tail * dt
        skip = heads[2].reshape(1, H, 1)
        (state,) = call(
            state_kernel, "chunk_state", chunks, [x_spec, b_spec, row_spec],
            [(state_spec, shape((chunks, DI, STATE), bf16))], small_flops, a, a, w,
        )
        weights = chunk_weights(last[:, :, 0], seqs, shards)
        hin = exchange(state, seqs, weights, shards, "imjnbh,jbnhx->ibmhx")
        (inner,) = call(
            inner_kernel, "inner", chunks, [x_spec, b_spec, c_spec, row_spec, row_spec],
            [(x_spec, shape((rows, DI)))], inner_flops // 3, a, a, a, cum, dt,
        )
        (y,) = call(
            carry_kernel, "carry", chunks,
            [x_spec, x_spec, c_spec, row_spec, one_spec, state_spec],
            [(x_spec, shape((rows, DI), bf16))], small_flops, inner, a, a, cum, skip, hin,
        )
        yf, zf = y.astype(f32), z.astype(f32)
        q = yf * (zf * jax.nn.sigmoid(zf))
        rs2 = rms_scale(q)
        nrm = (q * rs2 * g2).astype(bf16)
        saved.append((hidden, rs1, u, y, z, padded, pa, a, pre, dt, lam, rate, cum, last, w, skip, weights, hin, rs2, nrm))
        hidden = hidden + dot(nrm, out_mats[i], 1, 0)

    grad = cotangent.reshape(rows, D)
    big_grads = [None] * LAYERS
    small_grads = [None] * LAYERS
    for i in reversed(range(LAYERS)):
        (h, rs1, u, y, z, padded, pa, a, pre, dt, lam, rate, cum, last, w, skip, weights, hin, rs2, nrm) = saved[i]
        g1, g2 = gains_all[i, :D], gains_all[i, D:]
        taps = taps_all[i]
        go = grad.astype(bf16)
        gn = dot(go, out_mats[i], 1, 1)
        yf, zf = y.astype(f32), z.astype(f32)
        gate = zf * jax.nn.sigmoid(zf)
        q = yf * gate
        v = gn * g2
        gq = rs2 * v - q * (rs2 * rs2 * rs2) * jnp.mean(v * q, axis=-1, keepdims=True)
        grad_g2 = jnp.sum(gn * q * rs2, axis=0)
        gz = (gq * yf * silu_slope(zf)).astype(bf16)
        gy = (gq * gate).astype(bf16)
        (gstate,) = call(
            back_state_kernel, "back_state", chunks, [x_spec, c_spec, row_spec],
            [(state_spec, shape((chunks, DI, STATE), bf16))], small_flops, gy, a, cum,
        )
        gs = exchange(gstate, seqs, weights, shards, "imjnbh,ibmhx->jbnhx")
        grad_out = dot(nrm, go, 0, 0).astype(bf16)
        grad_out = lax.psum_scatter(grad_out, "fsdp", scatter_dimension=0, tiled=True)
        grad_out = lax.psum(grad_out, "seq").astype(f32)
        rows_shape = shape((chunks, H, SPAN))
        gx, gcb, row_pair, col_pair, gskip = call(
            back_inner_kernel, "back_inner", chunks,
            [x_spec, x_spec, b_spec, c_spec, row_spec, row_spec, one_spec],
            [
                (x_spec, shape((rows, DI))), (gcb_spec, shape((chunks, SPAN, SPAN))),
                (row_spec, rows_shape), (row_spec, rows_shape), (row_spec, rows_shape),
            ],
            inner_flops, a, gy, a, a, cum, dt, skip,
        )
        gx, gb, gc_state, carry, dw, cross = call(
            back_carry_kernel, "back_carry", chunks,
            [x_spec, x_spec, x_spec, b_spec, c_spec, row_spec, row_spec, state_spec, state_spec],
            [
                (x_spec, shape((rows, DI))), (bc_out_spec, shape((rows, STATE))),
                (bc_out_spec, shape((rows, STATE))), (row_spec, rows_shape), (row_spec, rows_shape),
                (cross_spec, shape((chunks, H, STATE))),
            ],
            4 * small_flops, gx, a, gy, a, a, cum, w, hin, gs,
        )
        gcb_b = gcb.astype(bf16)
        b_act = a[:, DI : DI + STATE].reshape(chunks, SPAN, STATE)
        c_act = a[:, DI + STATE :].reshape(chunks, SPAN, STATE)
        gc_state = gc_state + jnp.einsum(
            "gts,gsn->gtn", gcb_b, b_act, preferred_element_type=f32
        ).reshape(rows, STATE)
        gb = gb + jnp.einsum(
            "gts,gtn->gsn", gcb_b, c_act, preferred_element_type=f32
        ).reshape(rows, STATE)

        tail_sum = w * dw
        through = jnp.exp(last) * jnp.sum(cross, axis=2, keepdims=True)
        later = row_pair - dt * col_pair + carry - tail_sum
        glam = jnp.einsum("ght,st->ghs", later, upper, precision=highest)
        glam = glam + jnp.sum(tail_sum, axis=2, keepdims=True) + through
        gdt = col_pair + jnp.exp(last - cum) * dw + rate[:, None] * glam
        gr = gdt * jax.nn.sigmoid(pre)
        grad_heads = jnp.stack(
            [
                jnp.sum(gr, axis=(0, 2)),
                jnp.sum(glam * lam, axis=(0, 2)),
                jnp.sum(gskip, axis=(0, 2)),
            ]
        )
        gr_tok = gr.transpose(0, 2, 1).reshape(rows, H).astype(bf16)

        ga = jnp.concatenate([gx, gb, gc_state], axis=1)
        gpa = (ga * silu_slope(pa)).reshape(seqs, toks, CH)
        halo = lax.ppermute(gpa[:, :rim, :], "seq", left)
        gpad = jnp.concatenate([gpa, halo], axis=1)
        gc = jnp.zeros((), f32)
        grad_taps = []
        for k in range(TAPS):
            gc = gc + gpad[:, rim - k : rim - k + toks, :] * taps[k]
            grad_taps.append(jnp.sum(gpa * padded[:, k : k + toks, :].astype(f32), axis=(0, 1)))
        grad_taps.append(jnp.sum(gpa, axis=(0, 1)))
        gproj = jnp.concatenate([gz, gc.reshape(rows, CH).astype(bf16), gr_tok], axis=1)
        gu = dot(gproj, in_mats[i], 1, 1)
        grad_in = dot(u, gproj, 0, 0).astype(bf16)
        grad_in = lax.psum_scatter(grad_in, "fsdp", scatter_dimension=0, tiled=True)
        grad_in = lax.psum(grad_in, "seq").astype(f32)
        v = gu * g1
        mean_vh = jnp.mean(v * h, axis=-1, keepdims=True)
        grad_g1 = jnp.sum(gu * h * rs1, axis=0)
        grad = grad + rs1 * v - h * (rs1 * rs1 * rs1) * mean_vh
        big_grads[i] = (grad_in, grad_out)
        small_grads[i] = jnp.concatenate(
            [grad_g1, grad_g2, jnp.stack(grad_taps).reshape(-1), grad_heads.reshape(-1)]
        )

    small = lax.psum(jnp.stack(small_grads), ("seq", "fsdp"))
    size_a = D + DI
    size_b = size_a + (TAPS + 1) * CH
    own_gains = gains.shape[1]
    own_taps = conv_taps.shape[2]
    own_heads = head_params.shape[2]
    grads = (
        lax.dynamic_slice_in_dim(small[:, :size_a], fsdp_index * own_gains, own_gains, 1),
        jnp.stack([g[0] for g in big_grads]),
        lax.dynamic_slice_in_dim(
            small[:, size_a:size_b].reshape(LAYERS, TAPS + 1, CH), fsdp_index * own_taps, own_taps, 2
        ),
        lax.dynamic_slice_in_dim(
            small[:, size_b:].reshape(LAYERS, 3, H), fsdp_index * own_heads, own_heads, 2
        ),
        jnp.stack([g[1] for g in big_grads]),
    )
    results = [hidden.reshape(seqs, toks, D), grad.reshape(seqs, toks, D)]
    for kind in range(5):
        results.extend(
            adam_step(
                masters[kind], firsts[kind], seconds[kind], grads[kind],
                learn_rates[kind], weight_decays[kind],
            )
        )
    return tuple(results)


def solution(mesh):
    tokens = P("fsdp", "seq", None)
    per_kind = (P(None, "fsdp"), P(None, "fsdp", None), P(None, None, "fsdp"), P(None, None, "fsdp"), P(None, "fsdp", None))
    specs = (tokens, tokens) + tuple(s for s in per_kind for _ in range(3))
    return jax.shard_map(local, mesh=mesh, in_specs=specs, out_specs=specs, check_vma=False)
```

time: 2330 us -> 1020 us (0.44)
  local copies, waits for them, and re-layouts: 686 us -> 84.8 us
  other arithmetic: 479 us -> 108 us
  matrix products: 335 us -> 94 us
  waiting for transfers between devices: 628 us -> 472 us
  Pallas kernels: 0 us -> 112 us
    dynamic_update_slice x100 -> x0, local copies, waits for them, and re-layouts: 310 us -> none  [the longest x96 309 us: ssd_blocks(): lax.scan(jax.checkpoint(one_block), state_start, block_items)]
    dot_general x236 -> x26, matrix products: 335 us -> 94 us  [the longest x12 79 us: dot(): lax.dot_general(a, b, (((ca,), (cb,)), ((), ())), preferred_element_type=...]
    psum x1 -> x2, waiting for transfers between devices: 163 us -> 341 us  [the longest x1 222 us: local(): grad_in = lax.psum(grad_in, 'seq').astype(f32)]
    all_to_all x12 -> x6, waiting for transfers between devices: 167 us -> 11.5 us  [the longest x4 11.5 us: exchange(): lax.all_to_all(mixed, 'seq', split_axis=0, concat_axis=1, tiled=False)]
    another operation x133 -> x8, other arithmetic: 161 us -> 7.89 us
    reduce_scatter x6 -> x4, waiting for transfers between devices: 198 us -> 55.3 us  [the longest x2 55.3 us: local(): grad_in = lax.psum_scatter(grad_in, 'fsdp', scatter_dimension=0, tiled=True)]
    unnamed x16 -> x2, other arithmetic: 119 us -> 0.04 us
    pallas_call x0 -> x12, Pallas kernels: none -> 112 us  [call(): pl.pallas_call(kernel, grid=(chunks, H // GROUP), in_specs=ins, out_specs...]
  transfers between devices with their start and end apart: 27 -> 20, of which waited for: 14 -> 9; matrix products, arithmetic and copies ran while one was open for 26% -> 21% of each run, Pallas kernels for 0% -> 11%
where the time goes in v1:
time: 1020 us; the launch traced here: 1010 us
  waiting for transfers between devices  472 us (46%)
  Pallas kernels  112 us (11%)
  other arithmetic  108 us (11%)
  matrix products  94 us (9%)
  blocking collectives  85.1 us (8%)
  local copies, waits for them, and re-layouts  84.8 us (8%)
  starting transfers between devices  37.7 us (4%)
  between operations  16.7 us (2%)
    psum x1, waiting for transfers between devices, local(): grad_in = lax.psum(grad_in, 'seq').astype(f32)  222 us
    psum x1, waiting for transfers between devices, local(): small = lax.psum(jnp.stack(small_grads), ('seq', 'fsdp'))  119 us
    pallas_call x12, Pallas kernels, call(): pl.pallas_call(kernel, grid=(chunks, H // GROUP), in_specs=ins, out_specs...  112 us
    dot_general x12, matrix products, dot(): lax.dot_general(a, b, (((ca,), (cb,)), ((), ())), preferred_element_type=...  79 us
    all_gather x2, waiting for transfers between devices, local(): lax.all_gather(in_proj[i].astype(bf16), 'fsdp', axis=0, tiled=True)  58.8 us
    reduce_scatter x2, waiting for transfers between devices, local(): grad_in = lax.psum_scatter(grad_in, 'fsdp', scatter_dimension=0, tiled=True)  55.3 us
    all_gather x2, blocking collectives, chunk_weights(): lax.all_gather(totals.reshape(seqs, n, H), 'seq', axis=1, tiled=True)  45.3 us
    unnamed x319, local copies, waits for them, and re-layouts  35.1 us
  transfers between devices with their start and end apart: 20, of which 9 were waited for; matrix products, arithmetic and copies ran while one was open for 21% of the time, Pallas kernels for 11%

profile of v1, /device:TPU:0, one launch (start us, length us, event | category | flops | bytes accessed | tf_op | source)
XLA Modules:
  0.0 1010.7 jit_solution(17138192653906975034)
XLA Ops:
  18.8 6.4 all-gather.6
  28.1 51.2 %all-gather.12.cloned.1.call-done = bf16[1,1024,4384]{1,2,0:T(8,128)(2,1)} async-done(((bf16[1,256,4384]{1,2,0:T(8,128)(2,1)}), bf16[1,1024,4384]{1,2,0:T(8,128)(2,1)}) %all-gather.12.cloned.1.call-update) | async-done | bytes 8978448 | tf_op jit(solution)/shard_map/all_gather | solution.py:291
  79.3 6.2 fusion.14
  96.6 6.8 fusion.75
  104.9 5.8 chunk_state.2
  116.5 22.6 %all-gather.1 = f32[8,32,1]{1,2,0:T(1,128)S(1)} all-gather(f32[1,32,1]{1,2,0:T(1,128)S(1)} %copy.186), channel_id=3, replica_groups=mesh['seq'=8,'fsdp'=4] {'seq'}, dimensions={0}, use_global_device_ids=true | all-gather | bytes 1152 | tf_op jit(solution)/shard_map/all_gather | solution.py:233
  151.6 6.0 all-to-all-done.1
  173.4 7.6 all-gather.16.cloned.1.call-done
  181.0 6.5 fusion.17
  196.0 6.9 fusion.69
  216.1 22.7 %all-gather.4 = f32[8,32,1]{1,2,0:T(1,128)S(1)} all-gather(f32[1,32,1]{1,2,0:T(1,128)S(1)} %copy.204), channel_id=6, replica_groups=mesh['seq'=8,'fsdp'=4] {'seq'}, dimensions={0}, use_global_device_ids=true | all-gather | bytes 1152 | tf_op jit(solution)/shard_map/all_gather | solution.py:233
  277.1 5.8 multiply_reduce_fusion
  295.3 16.3 %all_to_all.32 = bf16[1,1,8,256,128]{4,3,1,0,2:T(8,128)(2,1)} all-to-all(bf16[1,1,8,256,128]{4,3,1,0,2:T(8,128)(2,1)S(1)} %bitcast.480), channel_id=1, replica_groups=mesh['seq'=8,'fsdp'=4] {'seq'}, dimensions={2} | all-to-all | bytes 1048576 | tf_op jit(solution)/shard_map/all_to_all | solution.py:222
  322.7 20.8 %back_inner.2 = (f32[256,2048]{1,0:T(8,128)S(1)}, f32[1,256,256]{2,1,0:T(8,128)S(1)}, f32[1,32,256]{2,1,0:T(8,128)S(1)}, f32[1,32,256]{2,1,0:T(8,128)S(1)}, f32[1,32,256]{2,1,0:T(8,128)S(1)}) custom-call(bf16[256,2304]{1,0:T(8,128)(2,1)S(1)} %copy.198.x_ref.b_ref.c_ref, bf16[256,2048]{1,0:T(8,128)(2,1)S(1)} %copy-done.5, ...), custom_call_target="tpu_custom_call" | custom-call | flops 2684354560 | bytes 7110784 | tf_op jit(solution)/shard_map/back_inner/pallas_call | solution.py:174
  350.2 15.5 %back_carry.2 = (f32[256,2048]{1,0:T(8,128)S(1)}, f32[256,128]{1,0:T(8,128)S(1)}, f32[256,128]{1,0:T(8,128)S(1)}, f32[1,32,256]{2,1,0:T(8,128)S(1)}, f32[1,32,25...) custom-call(f32[256,2048]{1,0:T(8,128)S(1)} %copy-done.10, bf16[256,2304]{1,0:T(8,128)(2,1)S(1)} %copy.198.x_ref.b_ref.c_ref, ...), custom_call_target="tpu_custom_call" | custom-call | flops 536870912 | bytes 10240000 | tf_op jit(solution)/shard_map/back_carry/pallas_call | solution.py:174
  379.1 6.4 fusion.45
  393.6 8.2 fusion.104
  401.9 7.3 multiply_reduce_fusion.6
  414.7 8.8 convolution_convert_fusion
  423.6 6.2 multiply_reduce_fusion.1
  438.9 17.1 %all_to_all.33 = bf16[1,1,8,256,128]{4,3,1,0,2:T(8,128)(2,1)S(1)} all-to-all(bf16[1,1,8,256,128]{4,3,1,0,2:T(8,128)(2,1)S(1)} %bitcast.481), channel_id=1, replica_groups=mesh['seq'=8,'fsdp'=4] {'seq'}, dimensions={2} | all-to-all | bytes 1048576 | tf_op jit(solution)/shard_map/all_to_all | solution.py:222
  462.7 20.9 %back_inner.3 = (f32[256,2048]{1,0:T(8,128)S(1)}, f32[1,256,256]{2,1,0:T(8,128)S(1)}, f32[1,32,256]{2,1,0:T(8,128)S(1)}, f32[1,32,256]{2,1,0:T(8,128)S(1)}, f32[1,32,256]{2,1,0:T(8,128)S(1)}) custom-call(bf16[256,2304]{1,0:T(8,128)(2,1)S(1)} %copy.180.x_ref.b_ref.c_ref, bf16[256,2048]{1,0:T(8,128)(2,1)S(1)} %copy.239.gy_ref, ...), custom_call_target="tpu_custom_call" | custom-call | flops 2684354560 | bytes 7110784 | tf_op jit(solution)/shard_map/back_inner/pallas_call | solution.py:174
  486.5 16.3 %back_carry.3 = (f32[256,2048]{1,0:T(8,128)S(1)}, f32[256,128]{1,0:T(8,128)S(1)}, f32[256,128]{1,0:T(8,128)S(1)}, f32[1,32,256]{2,1,0:T(8,128)S(1)}, f32[1,32,25...) custom-call(f32[256,2048]{1,0:T(8,128)S(1)} %copy-done.12, bf16[256,2304]{1,0:T(8,128)(2,1)S(1)} %copy.180.x_ref.b_ref.c_ref, ...), custom_call_target="tpu_custom_call" | custom-call | flops 536870912 | bytes 10240000 | tf_op jit(solution)/shard_map/back_carry/pallas_call | solution.py:174
  509.7 6.4 fusion.36
  524.2 8.5 fusion.105
  532.8 9.8 convolution_convert_fusion.1
  552.5 9.8 fusion.120
  563.5 55.3 %reduce-scatter.5.cloned.1.call-done = bf16[256,4384]{0,1:T(8,128)(2,1)} async-done(((bf16[1024,4384]{0,1:T(8,128)(2,1)}), bf16[256,4384]{0,1:T(8,128)(2,1)}) %reduce-scatter.5.cloned.1.call-update) | async-done | bytes 2244624 | tf_op jit(solution)/shard_map/reduce_scatter | solution.py:432
  626.8 119.4 %all-reduce.4.cloned.1.call-done = f32[2,14688]{1,0:T(2,128)} async-done(((f32[2,14688]{1,0:T(2,128)}), f32[2,14688]{1,0:T(2,128)}) %all-reduce.4.cloned.1.call-update) | async-done | bytes 117520 | tf_op jit(solution)/shard_map/psum | solution.py:443
  751.9 221.6 %all-reduce.6.cloned.1.call-done = (bf16[1,256,4384]{1,2,0:T(8,128)(2,1)}, bf16[1,256,4384]{1,2,0:T(8,128)(2,1)}, bf16[1,512,1024]{2,1,0:T(8,128)(2,1)}, bf16[1,512,1024]{2,1,0:T(8,128)(2,1)}) async-done(((bf16[1,256,4384]{1,2,0:T(8,128)(2,1)}, bf16[1,256,4384]{1,2,0:T(8,128)(2,1)}, bf16[1,512,1024]{2,1,0:T(8,128)(2,1)}, bf16[1,512,1024]{2,1,0:T(8,128)(2,1)}), (bf16[1,256,4384]{1,2,0:T(8,128)(2,1)}, ...) | async-done | bytes 6586384 | tf_op jit(solution)/shard_map/psum | solution.py:433
  973.5 23.6 %multiply_subtract_fusion = (f32[2,256,4384]{1,2,0:T(8,128)}, f32[2,256,4384]{1,2,0:T(8,128)}, f32[2,256,4384]{1,2,0:T(8,128)}) fusion(f32[2,256,4384]{1,2,0:T(8,128)} %param.22, bf16[1,256,4384]{1,2,0:T(8,128)(2,1)} %get-tuple-element.121, bf16[1,256,4384]{1,2,0:T(8,128)(2,1)} %get-tuple-element.122, f32[2,256,4384]{1,2,0:T(8,128)} %param.24, ...), kind=kLoop, calls=%fused_computation.18 | loop fusion | flops 38158336 | bytes 58359808 | tf_op jit(solution)/shard_map/sub | solution.py:212
  997.2 6.3 multiply_subtract_fusion.1
  (523 shorter events, 234.9 us)
Async XLA Ops:
  7.2 72.1 %all-gather.12.cloned.1.call-start = ((), (), s32[]{:S(2)}) async-start(), calls=%async_computation.17 | async-start | bytes 11223040 | tf_op jit(solution)/shard_map/all_gather | solution.py:291
  13.6 154.2 %all-gather.14.cloned.1.call-start = ((), (), s32[]{:S(2)}) async-start(), calls=%async_computation.18 | async-start | bytes 5242880 | tf_op jit(solution)/shard_map/all_gather | solution.py:294
  17.7 163.3 %all-gather.16.cloned.1.call-start = ((), (), s32[]{:S(2)}) async-start(), calls=%async_computation.19 | async-start | bytes 11223040 | tf_op jit(solution)/shard_map/all_gather | solution.py:291
  26.7 69.8 %copy-start.82 = (f32[2304]{0:T(1024)}, f32[2304]{0:T(1024)S(1)}, u32[]{:S(2)}) copy-start(f32[2304]{0:T(1024)S(1)} %get-tuple-element.117) | copy-start | bytes 27652
  28.1 152.9 %copy-start.116 = (f32[1,1024]{1,0:T(1,128)}, f32[1,1024]{1,0:T(1,128)S(1)}, u32[]{:S(2)}) copy-start(f32[1,1024]{1,0:T(1,128)S(1)} %get-tuple-element.168) | copy-start | bytes 12292
  89.0 5.7 collective-permute-start
  110.7 28.9 %all-to-all-start = ((bf16[1,1,8,256,128]{4,3,1,0,2:T(8,128)(2,1)}), bf16[1,1,8,256,128]{4,3,1,0,2:T(8,128)(2,1)S(1)}, u32[]{:S(2)}, u32[]{:S(2)}) async-start(bf16[1,1,8,256,128]{4,3,1,0,2:T(8,128)(2,1)} %bitcast.21), calls=%async_computation | async-start | bytes 1048576 | tf_op jit(solution)/shard_map/all_to_all | solution.py:222
  142.5 15.1 %all-to-all-start.1 = ((bf16[8,1,1,256,128]{4,3,2,1,0:T(8,128)(2,1)}), bf16[8,1,1,256,128]{4,3,2,1,0:T(8,128)(2,1)}, u32[]{:S(2)}, u32[]{:S(2)}) async-start(bf16[8,1,1,256,128]{4,3,2,1,0:T(8,128)(2,1)} %bitcast.25), calls=%async_computation.1 | async-start | bytes 1048576 | tf_op jit(solution)/shard_map/all_to_all | solution.py:227
  146.7 130.4 %all-gather.18.cloned.1.call-start = ((), (), s32[]{:S(2)}) async-start(), calls=%async_computation.20 | async-start | bytes 5242880 | tf_op jit(solution)/shard_map/all_gather | solution.py:294
  147.4 135.5 %copy-start.106 = (f32[1,2048]{1,0:T(1,128)}, f32[1,2048]{1,0:T(1,128)S(1)}, u32[]{:S(2)}) copy-start(f32[1,2048]{1,0:T(1,128)S(1)} %get-tuple-element.170) | copy-start | bytes 24580
  189.5 5.4 collective-permute-start.1
  210.3 29.1 %all-to-all-start.2 = ((bf16[1,1,8,256,128]{4,3,1,0,2:T(8,128)(2,1)}), bf16[1,1,8,256,128]{4,3,1,0,2:T(8,128)(2,1)S(1)}, u32[]{:S(2)}, u32[]{:S(2)}) async-start(bf16[1,1,8,256,128]{4,3,1,0,2:T(8,128)(2,1)} %bitcast.44), calls=%async_computation.2 | async-start | bytes 1048576 | tf_op jit(solution)/shard_map/all_to_all | solution.py:222
  246.0 14.6 %all-to-all-start.3 = ((bf16[8,1,1,256,128]{4,3,2,1,0:T(8,128)(2,1)}), bf16[8,1,1,256,128]{4,3,2,1,0:T(8,128)(2,1)S(1)}, u32[]{:S(2)}, u32[]{:S(2)}) async-start(bf16[8,1,1,256,128]{4,3,2,1,0:T(8,128)(2,1)} %bitcast.488), calls=%async_computation.3 | async-start | bytes 1048576 | tf_op jit(solution)/shard_map/all_to_all | solution.py:227
  249.5 314.0 %reduce-scatter.11.cloned.1.call-start = ((), (), s32[]{:S(2)}) async-start(), calls=%async_computation.16 | async-start | bytes 5242880 | tf_op jit(solution)/shard_map/reduce_scatter | solution.py:371
  316.3 31.1 %all-to-all-start.5 = ((bf16[8,1,1,256,128]{4,3,2,1,0:T(8,128)(2,1)}), bf16[8,1,1,256,128]{4,3,2,1,0:T(8,128)(2,1)S(1)}, u32[]{:S(2)}, u32[]{:S(2)}) async-start(bf16[8,1,1,256,128]{4,3,2,1,0:T(8,128)(2,1)} %bitcast.486), calls=%async_computation.5 | async-start | bytes 1048576 | tf_op jit(solution)/shard_map/all_to_all | solution.py:227
  319.9 243.5 %reduce-scatter.9.cloned.1.call-start = ((), (), s32[]{:S(2)}) async-start(), calls=%async_computation.15 | async-start | bytes 5242880 | tf_op jit(solution)/shard_map/reduce_scatter | solution.py:371
  387.3 5.8 collective-permute-start.2
  414.7 148.8 %reduce-scatter.7.cloned.1.call-start = ((), (), s32[]{:S(2)}) async-start(), calls=%async_computation.14 | async-start | bytes 11223040 | tf_op jit(solution)/shard_map/reduce_scatter | solution.py:432
  459.0 25.9 %all-to-all-start.7 = ((bf16[8,1,1,256,128]{4,3,2,1,0:T(8,128)(2,1)}), bf16[8,1,1,256,128]{4,3,2,1,0:T(8,128)(2,1)S(1)}, u32[]{:S(2)}, u32[]{:S(2)}) async-start(bf16[8,1,1,256,128]{4,3,2,1,0:T(8,128)(2,1)} %bitcast.487), calls=%async_computation.7 | async-start | bytes 1048576 | tf_op jit(solution)/shard_map/all_to_all | solution.py:227
  462.6 156.1 %reduce-scatter.5.cloned.1.call-start = ((), (), s32[]{:S(2)}) async-start(), calls=%async_computation.13 | async-start | bytes 11223040 | tf_op jit(solution)/shard_map/reduce_scatter | solution.py:432
  518.0 5.8 collective-permute-start.3
  542.7 203.5 %all-reduce.4.cloned.1.call-start = ((), (), s32[]{:S(2)}) async-start(), calls=%async_computation.12 | async-start | bytes 235520 | tf_op jit(solution)/shard_map/psum | solution.py:443
  563.1 410.4 %all-reduce.6.cloned.1.call-start = ((), (), s32[]{:S(2)}) async-start(), calls=%async_computation.21 | async-start | bytes 13172736 | tf_op jit(solution)/shard_map/psum | solution.py:433
  625.4 121.6 %copy-start.119 = (f32[2,3,8]{2,0,1:T(2,128)S(1)}, f32[2,3,8]{2,0,1:T(2,128)}, u32[]{:S(2)}) copy-start(f32[2,3,8]{2,0,1:T(2,128)} %param.28) | copy-start | bytes 580
  625.4 121.6 %copy-start.136 = (f32[2,3,8]{2,0,1:T(2,128)S(1)}, f32[2,3,8]{2,0,1:T(2,128)}, u32[]{:S(2)}) copy-start(f32[2,3,8]{2,0,1:T(2,128)} %param.30) | copy-start | bytes 580
  625.4 121.6 %copy-start.137 = (f32[2,3,8]{2,0,1:T(2,128)S(1)}, f32[2,3,8]{2,0,1:T(2,128)}, u32[]{:S(2)}) copy-start(f32[2,3,8]{2,0,1:T(2,128)} %param.29) | copy-start | bytes 580
  625.4 125.1 %copy-start.113 = (f32[2,768]{1,0:T(2,128)S(1)}, f32[2,768]{1,0:T(2,128)}, u32[]{:S(2)}) copy-start(f32[2,768]{1,0:T(2,128)} %param.19) | copy-start | bytes 18436
  625.4 125.1 %copy-start.122 = (f32[2,768]{1,0:T(2,128)S(1)}, f32[2,768]{1,0:T(2,128)}, u32[]{:S(2)}) copy-start(f32[2,768]{1,0:T(2,128)} %param.21) | copy-start | bytes 18436
  625.5 125.1 %copy-start.123 = (f32[2,768]{1,0:T(2,128)S(1)}, f32[2,768]{1,0:T(2,128)}, u32[]{:S(2)}) copy-start(f32[2,768]{1,0:T(2,128)} %param.20) | copy-start | bytes 18436
  625.5 125.7 %copy-start.95 = (f32[2,5,576]{2,0,1:T(2,128)S(1)}, f32[2,5,576]{2,0,1:T(2,128)}, u32[]{:S(2)}) copy-start(f32[2,5,576]{2,0,1:T(2,128)} %param.25) | copy-start | bytes 69124
  625.5 125.7 %copy-start.110 = (f32[2,5,576]{2,0,1:T(2,128)S(1)}, f32[2,5,576]{2,0,1:T(2,128)}, u32[]{:S(2)}) copy-start(f32[2,5,576]{2,0,1:T(2,128)} %param.27) | copy-start | bytes 69124
  625.5 125.7 %copy-start.111 = (f32[2,5,576]{2,0,1:T(2,128)S(1)}, f32[2,5,576]{2,0,1:T(2,128)}, u32[]{:S(2)}) copy-start(f32[2,5,576]{2,0,1:T(2,128)} %param.26) | copy-start | bytes 69124
  (145 other events, 1253.7 us)
Sparse Core Ops, SparseCore 0:
  13.8 65.5 all-gather.11
  81.5 34.4 all-gather.13
  118.1 62.8 all-gather.15
  183.0 34.4 all-gather.17
  277.2 42.6 reduce-scatter.10
  414.8 45.0 reduce-scatter.8
  463.1 75.5 reduce-scatter.6
  542.8 75.9 reduce-scatter.4
  624.9 121.2 all-reduce.3
  750.6 222.8 all-reduce.5

commit v2 on v1

--- a/solution.py
+++ b/solution.py
@@ -230,10 +230,11 @@
 
 def chunk_weights(totals, seqs, shards):
     n = totals.shape[0] // seqs
-    every = lax.all_gather(totals.reshape(seqs, n, H), "seq", axis=1, tiled=True)
     chunks = shards * n
     own = H // shards
-    mine = lax.dynamic_slice_in_dim(every, lax.axis_index("seq") * own, own, 2)
+    mine = lax.all_to_all(
+        totals.reshape(seqs, n, H), "seq", split_axis=2, concat_axis=1, tiled=True
+    )
     place = jnp.arange(chunks)
     between = (place[None, None, :] < place[:, None, None]) & (place[None, None, :] > place[None, :, None])
     logs = jnp.einsum("ijk,bkh->ijbh", between.astype(f32), mine, precision=highest)
@@ -266,7 +267,6 @@
     seconds = (gains_second, in_proj_second, conv_taps_second, head_params_second, out_proj_second)
     shards = lax.axis_size("seq")
     owners = lax.axis_size("fsdp")
-    fsdp_index = lax.axis_index("fsdp")
     seqs, toks, _ = hidden_in.shape
     rows = seqs * toks
     n = toks // SPAN
@@ -348,6 +348,7 @@
     grad = cotangent.reshape(rows, D)
     big_grads = [None] * LAYERS
     small_grads = [None] * LAYERS
+    before = None
     for i in reversed(range(LAYERS)):
         (h, rs1, u, y, z, padded, pa, a, pre, dt, lam, rate, cum, last, w, skip, weights, hin, rs2, nrm) = saved[i]
         g1, g2 = gains_all[i, :D], gains_all[i, D:]
@@ -369,7 +370,12 @@
         gs = exchange(gstate, seqs, weights, shards, "imjnbh,ibmhx->jbnhx")
         grad_out = dot(nrm, go, 0, 0).astype(bf16)
         grad_out = lax.psum_scatter(grad_out, "fsdp", scatter_dimension=0, tiled=True)
-        grad_out = lax.psum(grad_out, "seq").astype(f32)
+        grad_gate = dot(u, gz, 0, 0).astype(bf16)
+        grad_gate = lax.psum_scatter(grad_gate, "fsdp", scatter_dimension=0, tiled=True)
+        if before is not None:
+            grad_out, grad_gate, before = lax.optimization_barrier((grad_out, grad_gate, before))
+            big_grads[i + 1] += (before,)
+        grad_out, grad_gate = lax.psum((grad_out, grad_gate), "seq")
         rows_shape = shape((chunks, H, SPAN))
         gx, gcb, row_pair, col_pair, gskip = call(
             back_inner_kernel, "back_inner", chunks,
@@ -426,36 +432,49 @@
             gc = gc + gpad[:, rim - k : rim - k + toks, :] * taps[k]
             grad_taps.append(jnp.sum(gpa * padded[:, k : k + toks, :].astype(f32), axis=(0, 1)))
         grad_taps.append(jnp.sum(gpa, axis=(0, 1)))
-        gproj = jnp.concatenate([gz, gc.reshape(rows, CH).astype(bf16), gr_tok], axis=1)
-        gu = dot(gproj, in_mats[i], 1, 1)
-        grad_in = dot(u, gproj, 0, 0).astype(bf16)
+        gscan = jnp.concatenate([gc.reshape(rows, CH).astype(bf16), gr_tok], axis=1)
+        grad_in = dot(u, gscan, 0, 0).astype(bf16)
         grad_in = lax.psum_scatter(grad_in, "fsdp", scatter_dimension=0, tiled=True)
-        grad_in = lax.psum(grad_in, "seq").astype(f32)
+        grad_in, grad_out, grad_gate = lax.optimization_barrier((grad_in, grad_out, grad_gate))
+        before = lax.psum(grad_in, "seq")
+        gu = dot(jnp.concatenate([gz, gscan], axis=1), in_mats[i], 1, 1)
         v = gu * g1
         mean_vh = jnp.mean(v * h, axis=-1, keepdims=True)
         grad_g1 = jnp.sum(gu * h * rs1, axis=0)
         grad = grad + rs1 * v - h * (rs1 * rs1 * rs1) * mean_vh
-        big_grads[i] = (grad_in, grad_out)
+        big_grads[i] = (grad_out, grad_gate)
         small_grads[i] = jnp.concatenate(
             [grad_g1, grad_g2, jnp.stack(grad_taps).reshape(-1), grad_heads.reshape(-1)]
         )
 
-    small = lax.psum(jnp.stack(small_grads), ("seq", "fsdp"))
+    big_grads[0] += (before,)
+    small = jnp.stack(small_grads)
     size_a = D + DI
     size_b = size_a + (TAPS + 1) * CH
-    own_gains = gains.shape[1]
-    own_taps = conv_taps.shape[2]
-    own_heads = head_params.shape[2]
+
+    def by_owner(part):
+        part = part.reshape(part.shape[:-1] + (owners, part.shape[-1] // owners))
+        return jnp.moveaxis(part, -2, 0).reshape(owners, -1)
+
+    pieces = jnp.concatenate(
+        [
+            by_owner(small[:, :size_a]),
+            by_owner(small[:, size_a:size_b].reshape(LAYERS, TAPS + 1, CH)),
+            by_owner(small[:, size_b:].reshape(LAYERS, 3, H)),
+        ],
+        axis=1,
+    )
+    pieces = jnp.sum(lax.all_to_all(pieces, "fsdp", split_axis=0, concat_axis=0, tiled=True), axis=0)
+    pieces = jnp.broadcast_to(pieces, (shards,) + pieces.shape)
+    pieces = jnp.sum(lax.all_to_all(pieces, "seq", split_axis=0, concat_axis=0, tiled=True), axis=0)
+    size_a = gains.size
+    size_b = size_a + conv_taps.size
     grads = (
-        lax.dynamic_slice_in_dim(small[:, :size_a], fsdp_index * own_gains, own_gains, 1),
-        jnp.stack([g[0] for g in big_grads]),
-        lax.dynamic_slice_in_dim(
-            small[:, size_a:size_b].reshape(LAYERS, TAPS + 1, CH), fsdp_index * own_taps, own_taps, 2
-        ),
-        lax.dynamic_slice_in_dim(
-            small[:, size_b:].reshape(LAYERS, 3, H), fsdp_index * own_heads, own_heads, 2
-        ),
-        jnp.stack([g[1] for g in big_grads]),
+        pieces[:size_a].reshape(gains.shape),
+        jnp.stack([jnp.concatenate(g[1:], axis=1) for g in big_grads]).astype(f32),
+        pieces[size_a:size_b].reshape(conv_taps.shape),
+        pieces[size_b:].reshape(head_params.shape),
+        jnp.stack([g[0] for g in big_grads]).astype(f32),
     )
     results = [hidden.reshape(seqs, toks, D), grad.reshape(seqs, toks, D)]
     for kind in range(5):

time: 1020 us -> 1010 us (level)
  blocking collectives: 85.1 us -> 53.7 us
  starting transfers between devices: 37.7 us -> 59.5 us
  other arithmetic: 108 us -> 119 us
    psum x2 -> x4, waiting for transfers between devices: 341 us -> 265 us  [the longest x2 159 us: local(): before = lax.psum(grad_in, 'seq')]
    reduce_scatter x0 -> x2, waiting for transfers between devices: none -> 47.5 us  [local(): lax.psum_scatter(grad_gate, 'fsdp', scatter_dimension=0, tiled=True)]
    all_gather x2 -> x0, blocking collectives: 45.3 us -> none  [chunk_weights(): lax.all_gather(totals.reshape(seqs, n, H), 'seq', axis=1, tiled=True)]
    reduce_scatter x2, waiting for transfers between devices: 55.3 us -> 28.9 us  [local(): grad_in = lax.psum_scatter(grad_in, 'fsdp', scatter_dimension=0, tiled=True)]
    all_to_all x2, waiting for transfers between devices: 0.01 us -> 25.3 us  [exchange(): got = lax.all_to_all(send, 'seq', split_axis=1, concat_axis=0, tiled=False)]
    all_to_all x0 -> x4, starting transfers between devices: none -> 18.5 us  [the longest x2 11 us: chunk_weights(): lax.all_to_all(totals.reshape(seqs, n, H), 'seq', split_axis=2, concat_ax...]
    all_to_all x2, blocking collectives: 33.4 us -> 47.3 us  [exchange(): got = lax.all_to_all(send, 'seq', split_axis=1, concat_axis=0, tiled=False)]
    dot_general x12 -> x14, matrix products: 79 us -> 70.3 us  [dot(): lax.dot_general(a, b, (((ca,), (cb,)), ((), ())), preferred_element_type=...]
  transfers between devices with their start and end apart: 20 -> 28, of which waited for: 9 -> 17; matrix products, arithmetic and copies ran while one was open for 21% -> 23% of each run, Pallas kernels for 11% -> 11%
where the time goes in v2:
time: 1010 us; the launch traced here: 1000 us
  waiting for transfers between devices  466 us (46%)
  other arithmetic  119 us (12%)
  Pallas kernels  112 us (11%)
  local copies, waits for them, and re-layouts  91.7 us (9%)
  matrix products  85.2 us (8%)
  starting transfers between devices  59.5 us (6%)
  blocking collectives  53.7 us (5%)
  between operations  16.5 us (2%)
    psum x2, waiting for transfers between devices, local(): before = lax.psum(grad_in, 'seq')  159 us
    pallas_call x12, Pallas kernels, call(): pl.pallas_call(kernel, grid=(chunks, H // GROUP), in_specs=ins, out_specs...  112 us
    psum x2, waiting for transfers between devices, local(): grad_out, grad_gate = lax.psum((grad_out, grad_gate), 'seq')  106 us
    dot_general x14, matrix products, dot(): lax.dot_general(a, b, (((ca,), (cb,)), ((), ())), preferred_element_type=...  70.3 us
    all_gather x2, waiting for transfers between devices, local(): lax.all_gather(in_proj[i].astype(bf16), 'fsdp', axis=0, tiled=True)  63 us
    reduce_scatter x2, waiting for transfers between devices, local(): lax.psum_scatter(grad_gate, 'fsdp', scatter_dimension=0, tiled=True)  47.5 us
    all_to_all x2, blocking collectives, exchange(): got = lax.all_to_all(send, 'seq', split_axis=1, concat_axis=0, tiled=False)  47.3 us
    unnamed x333, local copies, waits for them, and re-layouts  42.8 us
  transfers between devices with their start and end apart: 28, of which 17 were waited for; matrix products, arithmetic and copies ran while one was open for 23% of the time, Pallas kernels for 11%

profile of v2, /device:TPU:0, one launch (start us, length us, event | category | flops | bytes accessed | tf_op | source)
XLA Modules:
  0.0 1003.7 jit_solution(12173942636534212290)
XLA Ops:
  18.8 6.4 all-gather.4
  27.6 51.7 %all-gather.10.cloned.1.call-done = bf16[1,1024,4384]{1,2,0:T(8,128)(2,1)} async-done(((bf16[1,256,4384]{1,2,0:T(8,128)(2,1)}), bf16[1,1024,4384]{1,2,0:T(8,128)(2,1)}) %all-gather.10.cloned.1.call-update) | async-done | bytes 8978448 | tf_op jit(solution)/shard_map/all_gather | solution.py:291
  79.3 6.2 fusion.14
  101.1 6.3 fusion.75
  114.0 6.3 all-to-all-start
  121.2 12.7 %all-to-all-done = bf16[1,1,8,256,128]{4,3,1,0,2:T(8,128)(2,1)S(1)} async-done(((bf16[1,1,8,256,128]{4,3,1,0,2:T(8,128)(2,1)}), bf16[1,1,8,256,128]{4,3,1,0,2:T(8,128)(2,1)S(1)}, u32[]{:S(2)}, u32[]{:S(2)}) %all-to-all-start) | async-done | bytes 524320 | tf_op jit(solution)/shard_map/all_to_all | solution.py:222
  145.8 8.5 all-to-all-done.2
  169.7 11.2 %all-gather.14.cloned.1.call-done = bf16[1,1024,4384]{1,2,0:T(8,128)(2,1)} async-done(((bf16[1,256,4384]{1,2,0:T(8,128)(2,1)}), bf16[1,1024,4384]{1,2,0:T(8,128)(2,1)}) %all-gather.14.cloned.1.call-update) | async-done | bytes 8978448 | tf_op jit(solution)/shard_map/all_gather | solution.py:291
  203.5 6.8 fusion.69
  217.7 6.7 all-to-all-start.3
  225.3 12.7 %all-to-all-done.3 = bf16[1,1,8,256,128]{4,3,1,0,2:T(8,128)(2,1)S(1)} async-done(((bf16[1,1,8,256,128]{4,3,1,0,2:T(8,128)(2,1)}), bf16[1,1,8,256,128]{4,3,1,0,2:T(8,128)(2,1)S(1)}, u32[]{:S(2)}, u32[]{:S(2)}) %all-to-all-start.3) | async-done | bytes 524320 | tf_op jit(solution)/shard_map/all_to_all | solution.py:222
  253.8 8.2 all-to-all-done.5
  301.9 17.0 %all_to_all.105 = bf16[1,1,8,256,128]{4,3,1,0,2:T(8,128)(2,1)} all-to-all(bf16[1,1,8,256,128]{4,3,1,0,2:T(8,128)(2,1)S(1)} %bitcast.498), channel_id=1, replica_groups=mesh['seq'=8,'fsdp'=4] {'seq'}, dimensions={2} | all-to-all | bytes 1048576 | tf_op jit(solution)/shard_map/all_to_all | solution.py:222
  330.2 20.8 %back_inner.2 = (f32[256,2048]{1,0:T(8,128)S(1)}, f32[1,256,256]{2,1,0:T(8,128)S(1)}, f32[1,32,256]{2,1,0:T(8,128)S(1)}, f32[1,32,256]{2,1,0:T(8,128)S(1)}, f32[1,32,256]{2,1,0:T(8,128)S(1)}) custom-call(bf16[256,2304]{1,0:T(8,128)(2,1)S(1)} %copy.527.x_ref.b_ref.c_ref, bf16[256,2048]{1,0:T(8,128)(2,1)S(1)} %copy-done.5, ...), custom_call_target="tpu_custom_call" | custom-call | flops 2684354560 | bytes 7110784 | tf_op jit(solution)/shard_map/back_inner/pallas_call | solution.py:174
  357.7 15.5 %back_carry.2 = (f32[256,2048]{1,0:T(8,128)S(1)}, f32[256,128]{1,0:T(8,128)S(1)}, f32[256,128]{1,0:T(8,128)S(1)}, f32[1,32,256]{2,1,0:T(8,128)S(1)}, f32[1,32,25...) custom-call(f32[256,2048]{1,0:T(8,128)S(1)} %copy-done.10, bf16[256,2304]{1,0:T(8,128)(2,1)S(1)} %copy.527.x_ref.b_ref.c_ref, ...), custom_call_target="tpu_custom_call" | custom-call | flops 536870912 | bytes 10240000 | tf_op jit(solution)/shard_map/back_carry/pallas_call | solution.py:174
  386.0 8.2 fusion.45
  403.3 9.2 fusion.120
  417.4 7.3 multiply_reduce_fusion.6
  449.4 30.2 %all_to_all.106 = bf16[1,1,8,256,128]{4,3,1,0,2:T(8,128)(2,1)S(1)} all-to-all(bf16[1,1,8,256,128]{4,3,1,0,2:T(8,128)(2,1)S(1)} %bitcast.499), channel_id=1, replica_groups=mesh['seq'=8,'fsdp'=4] {'seq'}, dimensions={2} | all-to-all | bytes 1048576 | tf_op jit(solution)/shard_map/all_to_all | solution.py:222
  486.3 20.9 %back_inner.3 = (f32[256,2048]{1,0:T(8,128)S(1)}, f32[1,256,256]{2,1,0:T(8,128)S(1)}, f32[1,32,256]{2,1,0:T(8,128)S(1)}, f32[1,32,256]{2,1,0:T(8,128)S(1)}, f32[1,32,256]{2,1,0:T(8,128)S(1)}) custom-call(bf16[256,2304]{1,0:T(8,128)(2,1)S(1)} %copy.509.x_ref.b_ref.c_ref, bf16[256,2048]{1,0:T(8,128)(2,1)S(1)} %copy.568.gy_ref, ...), custom_call_target="tpu_custom_call" | custom-call | flops 2684354560 | bytes 7110784 | tf_op jit(solution)/shard_map/back_inner/pallas_call | solution.py:174
  510.3 16.3 %back_carry.3 = (f32[256,2048]{1,0:T(8,128)S(1)}, f32[256,128]{1,0:T(8,128)S(1)}, f32[256,128]{1,0:T(8,128)S(1)}, f32[1,32,256]{2,1,0:T(8,128)S(1)}, f32[1,32,25...) custom-call(f32[256,2048]{1,0:T(8,128)S(1)} %copy-done.12, bf16[256,2304]{1,0:T(8,128)(2,1)S(1)} %copy.509.x_ref.b_ref.c_ref, ...), custom_call_target="tpu_custom_call" | custom-call | flops 536870912 | bytes 10240000 | tf_op jit(solution)/shard_map/back_carry/pallas_call | solution.py:174
  533.6 8.3 fusion.36
  554.2 9.3 fusion.121
  577.6 7.7 fusion.136
  590.2 10.2 %reduce-scatter.9.cloned.1.call-done = bf16[512,1024]{1,0:T(8,128)(2,1)} async-done(((bf16[2048,1024]{1,0:T(8,128)(2,1)}), bf16[512,1024]{1,0:T(8,128)(2,1)}) %reduce-scatter.9.cloned.1.call-update) | async-done | bytes 1048592 | tf_op jit(solution)/shard_map/reduce_scatter | solution.py:372
  600.4 47.5 %reduce-scatter.11.cloned.1.call-done = bf16[256,2048]{0,1:T(8,128)(2,1)} async-done(((bf16[1024,2048]{0,1:T(8,128)(2,1)}), bf16[256,2048]{0,1:T(8,128)(2,1)}) %reduce-scatter.11.cloned.1.call-update) | async-done | bytes 1048592 | tf_op jit(solution)/shard_map/reduce_scatter | solution.py:374
  647.9 84.9 %all-reduce.7.cloned.1.call-done = bf16[256,2336]{0,1:T(8,128)(2,1)} async-done(((bf16[256,2336]{0,1:T(8,128)(2,1)}), bf16[256,2336]{0,1:T(8,128)(2,1)}) %all-reduce.7.cloned.1.call-update) | async-done | bytes 1196048 | tf_op jit(solution)/shard_map/psum | solution.py:439
  758.1 25.5 %reduce-scatter.7.cloned.1.call-done = bf16[256,2336]{0,1:T(8,128)(2,1)} async-done(((bf16[1024,2336]{0,1:T(8,128)(2,1)}), bf16[256,2336]{0,1:T(8,128)(2,1)}) %reduce-scatter.7.cloned.1.call-update) | async-done | bytes 1196048 | tf_op jit(solution)/shard_map/reduce_scatter | solution.py:437
  783.6 105.9 %all-reduce.11.cloned.1.call-done = (bf16[512,1024]{1,0:T(8,128)(2,1)}, bf16[256,2048]{0,1:T(8,128)(2,1)}) async-done(((bf16[512,1024]{1,0:T(8,128)(2,1)}, bf16[256,2048]{0,1:T(8,128)(2,1)}), (bf16[512,1024]{1,0:T(8,128)(2,1)}, bf16[256,2048]{0,1:T(8,128)(2,1)})) %all-reduce.11.cloned.1.call-update) | async-done | bytes 2097168 | tf_op jit(solution)/shard_map/psum | solution.py:378
  889.5 9.6 multiply_subtract_fusion.1
  899.1 74.5 %all-reduce.9.cloned.1.call-done = bf16[256,2336]{0,1:T(8,128)(2,1)} async-done(((bf16[256,2336]{0,1:T(8,128)(2,1)}), bf16[256,2336]{0,1:T(8,128)(2,1)}) %all-reduce.9.cloned.1.call-update) | async-done | bytes 1196048 | tf_op jit(solution)/shard_map/psum | solution.py:439
  975.0 21.7 %multiply_subtract_fusion = (f32[2,256,4384]{1,2,0:T(8,128)}, f32[2,256,4384]{1,2,0:T(8,128)}, f32[2,256,4384]{1,2,0:T(8,128)}) fusion(f32[2,256,4384]{1,2,0:T(8,128)} %param.22, bf16[1,256,4384]{1,2,0:T(8,128)(2,1)S(1)} %maximum_bitcast_fusion.1, bf16[1,256,4384]{1,2,0:T(8,128)(2,1)S(1)} %maximum_bitcast_fusion, f32[2,256,4384]{1,2,0:T(8,128)} %param.24, ...), kind=kLoop, calls=%fused_computation.16 | loop fusion | flops 38158336 | bytes 58359808 | tf_op jit(solution)/shard_map/sub | solution.py:212
  (575 shorter events, 292.9 us)
Async XLA Ops:
  7.2 72.1 %all-gather.10.cloned.1.call-start = ((), (), s32[]{:S(2)}) async-start(), calls=%async_computation.26 | async-start | bytes 11223040 | tf_op jit(solution)/shard_map/all_gather | solution.py:291
  13.6 150.8 %all-gather.12.cloned.1.call-start = ((), (), s32[]{:S(2)}) async-start(), calls=%async_computation.27 | async-start | bytes 5242880 | tf_op jit(solution)/shard_map/all_gather | solution.py:294
  17.7 163.3 %all-gather.14.cloned.1.call-start = ((), (), s32[]{:S(2)}) async-start(), calls=%async_computation.28 | async-start | bytes 11223040 | tf_op jit(solution)/shard_map/all_gather | solution.py:291
  26.2 177.3 %copy-start.88 = (f32[2304]{0:T(1024)}, f32[2304]{0:T(1024)S(1)}, u32[]{:S(2)}) copy-start(f32[2304]{0:T(1024)S(1)} %get-tuple-element.198) | copy-start | bytes 27652
  26.2 177.3 %copy-start.89 = (f32[2304]{0:T(1024)}, f32[2304]{0:T(1024)S(1)}, u32[]{:S(2)}) copy-start(f32[2304]{0:T(1024)S(1)} %get-tuple-element.199) | copy-start | bytes 27652
  26.2 177.3 %copy-start.90 = (f32[2304]{0:T(1024)}, f32[2304]{0:T(1024)S(1)}, u32[]{:S(2)}) copy-start(f32[2304]{0:T(1024)S(1)} %get-tuple-element.200) | copy-start | bytes 27652
  26.2 177.3 %copy-start.91 = (f32[2304]{0:T(1024)}, f32[2304]{0:T(1024)S(1)}, u32[]{:S(2)}) copy-start(f32[2304]{0:T(1024)S(1)} %get-tuple-element.201) | copy-start | bytes 27652
  87.9 26.0 %all-to-all-start.1 = ((f32[1,1,32]{1,0,2:T(1,128)}), f32[1,1,32]{1,0,2:T(1,128)S(1)}, u32[]{:S(2)}, u32[]{:S(2)}) async-start(f32[1,1,32]{1,0,2:T(1,128)} %bitcast.22), calls=%async_computation.1 | async-start | bytes 32768 | tf_op jit(solution)/shard_map/all_to_all | solution.py:235
  95.3 5.4 collective-permute-start
  114.0 19.9 %all-to-all-start = ((bf16[1,1,8,256,128]{4,3,1,0,2:T(8,128)(2,1)}), bf16[1,1,8,256,128]{4,3,1,0,2:T(8,128)(2,1)S(1)}, u32[]{:S(2)}, u32[]{:S(2)}) async-start(bf16[1,1,8,256,128]{4,3,1,0,2:T(8,128)(2,1)} %bitcast.21), calls=%async_computation | async-start | bytes 1048576 | tf_op jit(solution)/shard_map/all_to_all | solution.py:222
  136.8 17.5 %all-to-all-start.2 = ((bf16[8,1,1,256,128]{4,3,2,1,0:T(8,128)(2,1)}), bf16[8,1,1,256,128]{4,3,2,1,0:T(8,128)(2,1)}, u32[]{:S(2)}, u32[]{:S(2)}) async-start(bf16[8,1,1,256,128]{4,3,2,1,0:T(8,128)(2,1)} %bitcast.26), calls=%async_computation.2 | async-start | bytes 1048576 | tf_op jit(solution)/shard_map/all_to_all | solution.py:227
  140.9 138.4 %all-gather.16.cloned.1.call-start = ((), (), s32[]{:S(2)}) async-start(), calls=%async_computation.29 | async-start | bytes 5242880 | tf_op jit(solution)/shard_map/all_gather | solution.py:294
  189.6 28.1 %all-to-all-start.4 = ((f32[1,1,32]{1,0,2:T(1,128)}), f32[1,1,32]{1,0,2:T(1,128)S(1)}, u32[]{:S(2)}, u32[]{:S(2)}) async-start(f32[1,1,32]{1,0,2:T(1,128)} %bitcast.46), calls=%async_computation.4 | async-start | bytes 32768 | tf_op jit(solution)/shard_map/all_to_all | solution.py:235
  197.0 5.4 collective-permute-start.1
  217.7 20.3 %all-to-all-start.3 = ((bf16[1,1,8,256,128]{4,3,1,0,2:T(8,128)(2,1)}), bf16[1,1,8,256,128]{4,3,1,0,2:T(8,128)(2,1)S(1)}, u32[]{:S(2)}, u32[]{:S(2)}) async-start(bf16[1,1,8,256,128]{4,3,1,0,2:T(8,128)(2,1)} %bitcast.45), calls=%async_computation.3 | async-start | bytes 1048576 | tf_op jit(solution)/shard_map/all_to_all | solution.py:222
  244.5 17.5 %all-to-all-start.5 = ((bf16[8,1,1,256,128]{4,3,2,1,0:T(8,128)(2,1)}), bf16[8,1,1,256,128]{4,3,2,1,0:T(8,128)(2,1)S(1)}, u32[]{:S(2)}, u32[]{:S(2)}) async-start(bf16[8,1,1,256,128]{4,3,2,1,0:T(8,128)(2,1)} %bitcast.503), calls=%async_computation.5 | async-start | bytes 1048576 | tf_op jit(solution)/shard_map/all_to_all | solution.py:227
  248.2 136.2 %reduce-scatter.15.cloned.1.call-start = ((), (), s32[]{:S(2)}) async-start(), calls=%async_computation.22 | async-start | bytes 5242880 | tf_op jit(solution)/shard_map/reduce_scatter | solution.py:372
  279.1 105.4 %reduce-scatter.17.cloned.1.call-start = ((), (), s32[]{:S(2)}) async-start(), calls=%async_computation.23 | async-start | bytes 5242880 | tf_op jit(solution)/shard_map/reduce_scatter | solution.py:374
  323.6 31.3 %all-to-all-start.7 = ((bf16[8,1,1,256,128]{4,3,2,1,0:T(8,128)(2,1)}), bf16[8,1,1,256,128]{4,3,2,1,0:T(8,128)(2,1)S(1)}, u32[]{:S(2)}, u32[]{:S(2)}) async-start(bf16[8,1,1,256,128]{4,3,2,1,0:T(8,128)(2,1)} %bitcast.502), calls=%async_computation.7 | async-start | bytes 1048576 | tf_op jit(solution)/shard_map/all_to_all | solution.py:227
  327.3 220.6 %all-reduce.13.cloned.1.call-start = ((), (), s32[]{:S(2)}) async-start(), calls=%async_computation.31 | async-start | bytes 4194304 | tf_op jit(solution)/shard_map/psum | solution.py:378
  384.5 166.8 %reduce-scatter.13.cloned.1.call-start = ((), (), s32[]{:S(2)}) async-start(), calls=%async_computation.21 | async-start | bytes 5980160 | tf_op jit(solution)/shard_map/reduce_scatter | solution.py:437
  396.1 5.8 collective-permute-start.2
  416.2 184.2 %reduce-scatter.9.cloned.1.call-start = ((), (), s32[]{:S(2)}) async-start(), calls=%async_computation.19 | async-start | bytes 5242880 | tf_op jit(solution)/shard_map/reduce_scatter | solution.py:372
  429.8 218.1 %reduce-scatter.11.cloned.1.call-start = ((), (), s32[]{:S(2)}) async-start(), calls=%async_computation.20 | async-start | bytes 5242880 | tf_op jit(solution)/shard_map/reduce_scatter | solution.py:374
  482.6 26.0 %all-to-all-start.9 = ((bf16[8,1,1,256,128]{4,3,2,1,0:T(8,128)(2,1)}), bf16[8,1,1,256,128]{4,3,2,1,0:T(8,128)(2,1)S(1)}, u32[]{:S(2)}, u32[]{:S(2)}) async-start(bf16[8,1,1,256,128]{4,3,2,1,0:T(8,128)(2,1)} %bitcast.76), calls=%async_computation.9 | async-start | bytes 1048576 | tf_op jit(solution)/shard_map/all_to_all | solution.py:227
  486.1 246.6 %all-reduce.7.cloned.1.call-start = ((), (), s32[]{:S(2)}) async-start(), calls=%async_computation.24 | async-start | bytes 2392064 | tf_op jit(solution)/shard_map/psum | solution.py:439
  546.2 6.6 collective-permute-start.3
  551.3 232.3 %reduce-scatter.7.cloned.1.call-start = ((), (), s32[]{:S(2)}) async-start(), calls=%async_computation.18 | async-start | bytes 5980160 | tf_op jit(solution)/shard_map/reduce_scatter | solution.py:437
  586.8 151.3 %all-to-all-start.10 = ((f32[4,1,7344]{2,1,0:T(1,128)}), f32[4,1,7344]{2,1,0:T(1,128)S(1)}, u32[]{:S(2)}, u32[]{:S(2)}) async-start(f32[4,1,7344]{2,1,0:T(1,128)} %copy.596), calls=%async_computation.10 | async-start | bytes 237568 | tf_op jit(solution)/shard_map/all_to_all | solution.py:467
  590.2 299.3 %all-reduce.11.cloned.1.call-start = ((), (), s32[]{:S(2)}) async-start(), calls=%async_computation.30 | async-start | bytes 4194304 | tf_op jit(solution)/shard_map/psum | solution.py:378
  739.2 12.4 %all-to-all-start.11 = ((f32[8,1,7344]{2,1,0:T(1,128)}), f32[8,1,7344]{2,1,0:T(1,128)S(1)}, u32[]{:S(2)}, u32[]{:S(2)}) async-start(f32[8,1,7344]{2,1,0:T(1,128)} %broadcast_in_dim.69), calls=%async_computation.11 | async-start | bytes 475136 | tf_op jit(solution)/shard_map/all_to_all | solution.py:469
  743.4 230.2 %all-reduce.9.cloned.1.call-start = ((), (), s32[]{:S(2)}) async-start(), calls=%async_computation.25 | async-start | bytes 2392064 | tf_op jit(solution)/shard_map/psum | solution.py:439
  (158 other events, 2348.9 us)
Sparse Core Ops, SparseCore 0:
  13.8 65.5 all-gather.9
  81.5 34.4 all-gather.11
  118.1 62.8 all-gather.13
  183.0 34.4 all-gather.15
  279.2 42.6 reduce-scatter.14
  325.0 44.4 reduce-scatter.16
  384.6 116.6 all-reduce.12
  504.4 46.8 reduce-scatter.12
  554.5 45.8 reduce-scatter.8
  603.3 44.4 reduce-scatter.10
  651.8 80.8 all-reduce.6
  735.9 47.6 reduce-scatter.6
  787.3 102.1 all-reduce.10
  892.9 80.6 all-reduce.8
